TPU v7x, 128 devices: a whole 4x4x4 slice. The times are simulated.
128 devices in a mesh: grp: 8 (over z_lo, x), tp: 16 (over z_hi, y, core).
Axes of the slice: x: 4, y: 4, z: 4 (z_hi: 2, z_lo: 2; z = z_hi * 2 + z_lo), core: 2. Of those that a mesh axis runs over, the one named last changes fastest.
Arguments:
- master: float32 [16, 720, 3, 2880], P('grp', 'tp'), may hold values from -0.109375 to 0.109375
- moment_one: float32 [16, 720, 3, 2880], P('grp', 'tp'), may hold values from -0.06 to 0.06
- moment_two: float32 [16, 720, 3, 2880], P('grp', 'tp'), may hold values from 1e-06 to 0.0001
- gradient: float32 [16, 720, 3, 2880], P('grp', 'tp'), may hold values from -0.3 to 0.3
- piece_owner: int32 [16], replicated, may hold values from 0 to 15, each once
- tokens: bfloat16 [4, 1024, 2880], P(None, 'grp', 'tp'), may hold values from -6 to 6
- routes: int32 [4, 1024, 2], P(None, 'grp'), may hold values from 0 to 3, all different within a row; in each aligned block of 128 rows (0 to 127, 128 to 255, ..., all dimensions but the last counted through in order) at most 96 rows name the same one
- mix_weight: float32 [4, 1024, 2], P(None, 'grp'), may hold values from 0.2 to 1
Outputs:
- decoded: bfloat16 [4, 1024, 2880], P(None, 'grp', 'tp')
Inputs may be any that keep to these rules, and one draw needn't show every extreme that they name: `routes`: within each aligned block of 128 rows (one step of one replica) the two choices of a token differ, and no expert is named more than 96 times; some expert is named exactly 96 times. A permutation; piece slot g stores row block piece_owner[g] % 4 of expert piece_owner[g] // 4.
All inputs are finite; a program needn't handle non-finite values.
Results may differ from a plain program's by a relative error of at most 0.0049.
The roundings to bfloat16 on the way count: a program that leaves them out, or rounds other values in their place, can miss the bound.
Values may be sent and summed in bfloat16 or wider, within the bound.
No kernel may reach another device: no remote copies, remote signals or barrier semaphores. Data moves between devices by JAX's collectives and lax.ppermute only.
A program may use at most 192 MiB of HBM per device.

v0:
```python
import jax
import jax.numpy as jnp
from jax import lax
from jax.sharding import PartitionSpec as P

D = 2880
EXPERTS = 4
TOP = 2
STEPS = 4
CAP = 96


learn_rate = 0.003
beta_one = 0.9
beta_two = 0.999
adam_eps = 1e-08
decay_rate = 0.1
bias_one = 1.0 - 0.9**20
bias_two = 1.0 - 0.999**20


def dispatch(chosen, experts, capacity):
    token_count, top_count = chosen.shape
    chosen_flat = chosen.reshape(-1)
    one_hot = (chosen_flat[:, None] == jnp.arange(experts, dtype=jnp.int32)[None, :]).astype(
        jnp.int32
    )
    earlier = jnp.cumsum(one_hot, axis=0, dtype=jnp.int32) - one_hot
    slot_of = jnp.sum(earlier * one_hot, axis=1, dtype=jnp.int32)
    slot_ids = chosen_flat * capacity + slot_of
    owner_rows = jnp.arange(token_count * top_count, dtype=jnp.int32) // top_count
    source_rows = jnp.zeros((experts * capacity,), jnp.int32).at[slot_ids].set(owner_rows)
    return (slot_ids, source_rows)


def shards(master, moment_one, moment_two, gradient, piece_owner, tokens, routes, mix_weight):
    moment_new = beta_one * moment_one + (1.0 - beta_one) * gradient
    second_new = beta_two * moment_two + (1.0 - beta_two) * gradient * gradient
    adjust = (
        moment_new / bias_one / (jnp.sqrt(second_new / bias_two) + adam_eps) + decay_rate * master
    )
    updated = (master - learn_rate * adjust).astype(jnp.bfloat16)
    piece_count = piece_owner.shape[0]
    inverse = (
        jnp.zeros((piece_count,), jnp.int32)
        .at[piece_owner]
        .set(jnp.arange(piece_count, dtype=jnp.int32))
    )
    every_piece = lax.all_gather(updated, "grp", axis=0, tiled=True)
    ordered = jnp.take(every_piece, inverse, axis=0)
    served = lax.all_to_all(ordered, "tp", split_axis=3, concat_axis=1, tiled=True)
    unit_count = served.shape[3]
    weights = served.reshape(EXPERTS, D, 3, unit_count)
    gate_weight = weights[:, :, 0, :]
    up_weight = weights[:, :, 1, :]
    down_weight = jnp.swapaxes(weights[:, :, 2, :], 1, 2)
    token_count = tokens.shape[1]
    outputs = []
    for step_index in range(STEPS):
        token_rows = lax.all_gather(tokens[step_index], "tp", axis=1, tiled=True)
        slot_ids, source_rows = dispatch(routes[step_index], EXPERTS, CAP)
        picked = jnp.take(token_rows, source_rows, axis=0).reshape(EXPERTS, CAP, D)
        gate = jnp.einsum("ecd,edf->ecf", picked, gate_weight, preferred_element_type=jnp.float32)
        upper = jnp.einsum("ecd,edf->ecf", picked, up_weight, preferred_element_type=jnp.float32)
        hidden = ((upper + 1.0) * gate * jax.nn.sigmoid(1.702 * gate)).astype(jnp.bfloat16)
        expert_out = jnp.einsum(
            "ecf,efd->ecd", hidden, down_weight, preferred_element_type=jnp.float32
        )
        gathered = jnp.take(expert_out.reshape(EXPERTS * CAP, D), slot_ids, axis=0)
        combined = jnp.sum(
            gathered.reshape(token_count, TOP, D) * mix_weight[step_index][:, :, None], axis=1
        )
        summed = lax.psum_scatter(combined, "tp", scatter_dimension=1, tiled=True)
        outputs.append(summed.astype(jnp.bfloat16))
    return jnp.stack(outputs)


def solution(mesh):
    return jax.shard_map(
        shards,
        mesh=mesh,
        in_specs=(
            P("grp", "tp", None, None),
            P("grp", "tp", None, None),
            P("grp", "tp", None, None),
            P("grp", "tp", None, None),
            P(),
            P(None, "grp", "tp"),
            P(None, "grp", None),
            P(None, "grp", None),
        ),
        out_specs=P(None, "grp", "tp"),
        check_vma=False,
    )
```

profile of v0, /device:TPU:24, one launch (start us, length us, event | category | flops | bytes accessed | tf_op | source)
XLA Modules:
  0.0 1021.4 jit_solution(9868437381473854114)
XLA Ops:
  6.5 8.6 subtract_convert_fusion
  16.1 141.8 %all-gather.6.cloned.1.call-done = bf16[16,45,3,2880]{3,1,2,0:T(8,128)(2,1)} async-done(((bf16[2,45,3,2880]{3,1,2,0:T(8,128)(2,1)}), bf16[16,45,3,2880]{3,1,2,0:T(8,128)(2,1)}) %all-gather.6.cloned.1.call-update) | async-done | bytes 12441616 | tf_op jit(solution)/shard_map/all_gather | solution.py:49
  157.9 11.8 %gather_fusion = bf16[16,45,3,2880]{3,1,2,0:T(8,128)(2,1)} fusion(bf16[16,45,3,2880]{3,1,2,0:T(8,128)(2,1)} %all-gather.6.cloned.1.call-done, s32[1024]{0:T(1024)S(1)} %pad_clamp_fusion.7), kind=kCustom, calls=%fused_computation.8 | custom fusion | bytes 24883264 | tf_op jit(solution)/shard_map/jit(_take)/gather | solution.py:50
  169.7 11.3 %broadcast_select_fusion = bf16[16,45,3,2880]{3,1,2,0:T(8,128)(2,1)} fusion(bf16[16,45,3,2880]{3,1,2,0:T(8,128)(2,1)} %gather_fusion, pred[16]{0:T(512)(128)(4,1)S(1)} %compare_and_fusion.8), kind=kLoop, calls=%fused_computation.14 | loop fusion | flops 6220800 | bytes 24883216 | tf_op jit(solution)/shard_map/jit(_take)/select_n | solution.py:50
  181.1 42.9 %copy.164 = bf16[16,45,3,2880]{1,0,2,3:T(8,128)(2,1)} copy(bf16[16,45,3,2880]{3,1,2,0:T(8,128)(2,1)} %broadcast_select_fusion) | data formatting | bytes 24883200 | tf_op jit(solution)/shard_map/jit(_take)/select_n | solution.py:50
  223.9 79.2 %reshape.412 = bf16[16,2,194400]{2,1,0:T(2,128)(2,1)} reshape(bf16[2880,3,16,45]{3,2,1,0:T(8,128)(2,1)} %bitcast.217) | data formatting | bytes 24883200
  303.2 7.2 all-to-all-start
  312.0 180.4 %all-gather.3 = bf16[1,128,2880]{1,0,2:T(2,128)(2,1)S(1)} all-gather(bf16[1,128,180]{1,0,2:T(2,128)(2,1)S(1)} %get-tuple-element.25), channel_id=5, replica_groups=mesh['grp'=8,'tp'=16] {'tp'}, dimensions={2}, use_global_device_ids=true | all-gather | bytes 783360 | tf_op jit(solution)/shard_map/all_gather | solution.py:60
  496.2 26.6 %all-gather.2 = bf16[1,128,2880]{1,0,2:T(2,128)(2,1)S(1)} all-gather(bf16[1,128,180]{1,0,2:T(2,128)(2,1)S(1)} %get-tuple-element.26), channel_id=4, replica_groups=mesh['grp'=8,'tp'=16] {'tp'}, dimensions={2}, use_global_device_ids=true | all-gather | bytes 783360 | tf_op jit(solution)/shard_map/all_gather | solution.py:60
  529.6 25.2 %all-gather.1 = bf16[1,128,2880]{1,0,2:T(2,128)(2,1)} all-gather(bf16[1,128,180]{1,0,2:T(2,128)(2,1)S(1)} %get-tuple-element.24), channel_id=3, replica_groups=mesh['grp'=8,'tp'=16] {'tp'}, dimensions={2}, use_global_device_ids=true | all-gather | bytes 783360 | tf_op jit(solution)/shard_map/all_gather | solution.py:60
  554.8 3.5 copy.177
  561.7 26.6 %all-gather = bf16[1,128,2880]{1,0,2:T(2,128)(2,1)} all-gather(bf16[1,128,180]{1,0,2:T(2,128)(2,1)S(1)} %get-tuple-element.23), channel_id=2, replica_groups=mesh['grp'=8,'tp'=16] {'tp'}, dimensions={2}, use_global_device_ids=true | all-gather | bytes 783360 | tf_op jit(solution)/shard_map/all_gather | solution.py:60
  588.3 3.5 copy.156
  595.5 3.5 gather_fusion.7
  599.0 3.5 gather_fusion.5
  602.5 3.5 gather_fusion.3
  606.0 3.4 gather_fusion.1
  618.1 109.4 %reshape.413 = bf16[2880,3,16,45]{3,2,1,0:T(8,128)(2,1)} reshape(bf16[16,2,194400]{2,1,0:T(2,128)(2,1)} %all-to-all-done) | data formatting | bytes 24883200
  727.4 45.3 %copy.166 = bf16[16,16,45,3,180]{4,2,1,0,3:T(8,128)(2,1)} copy(bf16[16,16,45,3,180]{2,0,3,4,1:T(8,128)(2,1)} %bitcast.216) | data formatting | bytes 24883200 | tf_op jit(solution)/shard_map/all_to_all | solution.py:51
  772.8 27.0 %reshape.241 = bf16[4,2880,3,180]{3,1,0,2:T(8,128)(2,1)} reshape(bf16[16,16,45,3,180]{4,2,1,0,3:T(8,128)(2,1)} %copy.166) | data formatting | bytes 24883200 | tf_op jit(solution)/shard_map/reshape | solution.py:53
  799.8 4.6 fusion.8
  804.4 10.1 fusion.12
  814.6 6.8 gather_fusion.8
  821.3 2.1 broadcast_select_fusion.5
  823.5 3.1 reshape.255
  826.6 7.4 multiply_reduce_fusion
  834.0 3.0 copy.195
  837.1 4.6 fusion.9
  841.7 10.1 fusion.13
  851.8 7.2 gather_fusion.6
  861.1 3.0 reshape.251
  864.1 7.4 multiply_reduce_fusion.1
  871.5 2.9 copy.187
  874.4 4.6 fusion.10
  879.0 10.1 fusion.14
  889.1 7.0 gather_fusion.4
  898.2 3.0 reshape.247
  901.2 7.4 multiply_reduce_fusion.2
  908.6 3.0 copy.179
  911.6 4.6 fusion.11
  916.2 10.1 fusion.15
  926.4 7.0 gather_fusion.2
  933.3 2.1 broadcast_select_fusion.8
  935.5 2.9 reshape.243
  938.4 6.2 multiply_reduce_fusion.3
  946.2 44.0 %fusion.102 = (f32[128,192]{0,1:T(8,128)S(1)}, f32[128,192]{0,1:T(8,128)S(1)}, f32[128,192]{0,1:T(8,128)S(1)}, f32[128,192]{0,1:T(8,128)S(1)}) fusion(f32[128,2880]{0,1:T(8,128)S(1)} %copy-done.8, f32[128,2880]{0,1:T(8,128)} %copy.187, f32[128,2880]{0,1:T(8,128)} %copy.179, f32[128,2880]{0,1:T(8,128)} %copy.171), kind=kCustom, calls=%all-reduce-scatter.4 | all-reduce-scatter fusion | flops 1572865 | bytes 6291968
  990.2 6.3 collective-permute-start.3
  997.9 8.0 collective-permute-start.2
  (159 shorter events, 43.5 us)
Async XLA Ops:
  6.5 8.6 copy-start.13
  6.5 9.3 copy-start.9
  6.5 151.4 %all-gather.6.cloned.1.call-start = ((), (), s32[]{:S(2)}) async-start(), calls=%async_computation.1 | async-start | bytes 15261696 | tf_op jit(solution)/shard_map/all_gather | solution.py:49
  303.2 7.2 copy-start.10
  303.2 314.9 %all-to-all-start = ((bf16[16,2,194400]{2,1,0:T(2,128)(2,1)}), bf16[16,2,194400]{2,1,0:T(2,128)(2,1)}, u32[]{:S(2)}, u32[]{:S(2)}) async-start(bf16[16,2,194400]{2,1,0:T(2,128)(2,1)} %reshape.412), calls=%async_computation | async-start | bytes 24887296 | tf_op jit(solution)/shard_map/all_to_all | solution.py:51
  310.4 185.7 %copy-start.11 = (f32[4,128,2]{1,2,0:T(2,128)S(1)}, f32[4,128,2]{1,2,0:T(2,128)}, u32[]{:S(2)}) copy-start(f32[4,128,2]{1,2,0:T(2,128)} %param.19) | copy-start | bytes 12292
  606.0 3.6 copy-start.1
  609.4 2.1 copy-start.2
  611.5 2.5 copy-start.4
  614.0 2.5 copy-start.5
  772.8 27.0 %copy-start.7 = (bf16[384,2880]{1,0:T(8,128)(2,1)S(1)}, bf16[384,2880]{1,0:T(8,128)(2,1)}, u32[]{:S(2)}) copy-start(bf16[384,2880]{1,0:T(8,128)(2,1)} %broadcast_select_fusion.1) | copy-start | bytes 6635524
  826.6 10.4 %copy-start.6 = (bf16[384,2880]{1,0:T(8,128)(2,1)S(1)}, bf16[384,2880]{1,0:T(8,128)(2,1)}, u32[]{:S(2)}) copy-start(bf16[384,2880]{1,0:T(8,128)(2,1)} %broadcast_select_fusion.2) | copy-start | bytes 6635524
  864.1 10.4 %copy-start.3 = (bf16[384,2880]{1,0:T(8,128)(2,1)S(1)}, bf16[384,2880]{1,0:T(8,128)(2,1)}, u32[]{:S(2)}) copy-start(bf16[384,2880]{1,0:T(8,128)(2,1)} %broadcast_select_fusion.3) | copy-start | bytes 6635524
  901.2 10.4 %copy-start = (bf16[384,2880]{1,0:T(8,128)(2,1)S(1)}, bf16[384,2880]{1,0:T(8,128)(2,1)}, u32[]{:S(2)}) copy-start(bf16[384,2880]{1,0:T(8,128)(2,1)} %broadcast_select_fusion.4) | copy-start | bytes 6635524
  938.4 7.8 copy-start.8
  946.2 50.3 %copy-start.12 = (u32[128]{0:T(128)S(1)}, u32[128]{0:T(128)}, u32[]{:S(2)}) copy-start(u32[128]{0:T(128)} %constant.107) | copy-start | bytes 1540
  990.2 19.5 %collective-permute-start.3 = (bf16[128,180]{0,1:T(8,128)(2,1)S(1)}, bf16[128,180]{0,1:T(8,128)(2,1)S(1)}, u32[]{:S(2)}, u32[]{:S(2)}) collective-permute-start(bf16[128,180]{0,1:T(8,128)(2,1)S(1)} %slice.120), channel_id=1, source_target_pairs={{0,1},{1,2},{2,3},{3,4},{4,5},{5,6},{6,7},{7,8},{8,9},{9,10},{10,1... | collective-permute-start | bytes 138248
  997.9 12.3 %collective-permute-start.2 = (bf16[128,180]{0,1:T(8,128)(2,1)S(1)}, bf16[128,180]{0,1:T(8,128)(2,1)S(1)}, u32[]{:S(2)}, u32[]{:S(2)}) collective-permute-start(bf16[128,180]{0,1:T(8,128)(2,1)S(1)} %slice.119), channel_id=1, source_target_pairs={{0,1},{1,2},{2,3},{3,4},{4,5},{5,6},{6,7},{7,8},{8,9},{9,10},{10,1... | collective-permute-start | bytes 138248
  1005.8 5.4 collective-permute-start.1
  1007.8 5.4 collective-permute-start
Sparse Core Ops, SparseCore 0:
  15.3 142.5 all-gather.5
where the time goes:
time: 1030 us; the launch traced here: 1020 us
  local copies, waits for them, and re-layouts  406 us (39%)
  blocking collectives  303 us (29%)
  waiting for transfers between devices  144 us (14%)
  other arithmetic  69.3 us (7%)
  matrix products  58.8 us (6%)
  starting transfers between devices  25.4 us (2%)
  between operations  14.9 us (1%)
    all_gather x4, blocking collectives, shards(): token_rows = lax.all_gather(tokens[step_index], 'tp', axis=1, tiled=True)  259 us
    unnamed x39, local copies, waits for them, and re-layouts  193 us
    all_gather x1, waiting for transfers between devices, shards(): every_piece = lax.all_gather(updated, 'grp', axis=0, tiled=True)  142 us
    all_to_all x1, local copies, waits for them, and re-layouts, shards(): lax.all_to_all(ordered, 'tp', split_axis=3, concat_axis=1, tiled=True)  45.3 us
    unnamed x1, blocking collectives  44 us
    select_n x1, local copies, waits for them, and re-layouts, shards(): ordered = jnp.take(every_piece, inverse, axis=0)  42.9 us
    dot_general x4, matrix products, shards(): jnp.einsum('ecf,efd->ecd', hidden, down_weight, preferred_element_type=jn...  40.4 us
    reduce_sum x4, other arithmetic, shards(): jnp.sum(gathered.reshape(token_count, TOP, D) * mix_weight[step_index][:,...  28.4 us
  transfers between devices with their start and end apart: 6, of which 3 were waited for; matrix products, arithmetic and copies ran while one was open for 5% of the time, Pallas kernels for 0%

commit v1 on v0

v1 whole, which is shorter than its diff:
```python
import functools

import jax
import jax.numpy as jnp
from jax import lax
from jax.experimental import pallas as pl
from jax.experimental.pallas import tpu as pltpu
from jax.sharding import Mesh
from jax.sharding import PartitionSpec as P

EXPERTS = 4
ROWS = 48
TOK = 512

learn_rate = 0.003
beta_one = 0.9
beta_two = 0.999
adam_eps = 1e-08
decay_rate = 0.1
bias_one = 1.0 - 0.9**20
bias_two = 1.0 - 0.999**20

bf16 = jnp.bfloat16
f32 = jnp.float32


def pack_kernel(w_ref, o_ref):
    lane = lax.broadcasted_iota(jnp.int32, (ROWS, 128), 1)

    def load(s, k, j):
        return w_ref[s, k, :, j * 128 : (j + 1) * 128].astype(f32)

    def roll(x, by):
        by = by % 128
        return x if by == 0 else pltpu.roll(x, by, 1)

    for j in range(8):
        for s in range(2):
            gate_b, up_b = load(s, 0, 16 + j), load(s, 1, 16 + j)
            for half in range(2):
                i = 2 * j + half
                gate, up, down = load(s, 0, i), load(s, 1, i), load(s, 2, i)
                for odd in range(2):
                    d = 2 * i + odd
                    off = 32 * (d % 4)
                    first = jnp.where(lane < 64, roll(gate, 64 * odd), roll(up, 64 - 64 * odd))
                    o_ref[d, 2 * s] = first.astype(bf16)
                    rest = jnp.where(lane < 96, roll(gate_b, 64 - off), roll(up_b, 96 - off))
                    second = jnp.where(lane < 64, roll(down, 64 * odd), rest)
                    o_ref[d, 2 * s + 1] = second.astype(bf16)
        down_0, down_1 = load(0, 2, 16 + j), load(1, 2, 16 + j)
        for q in range(4):
            last = jnp.where(lane < 32, roll(down_0, -32 * q), roll(down_1, 32 - 32 * q))
            o_ref[4 * j + q, 4] = jnp.where(lane < 64, last, 0.0).astype(bf16)


def expert_kernel(tab, mix_ref, x_ref, w0, w1a, w1b, w2a, w2b, w3a, w3b, own_ref, send_ref, wbuf, dbuf, acc, hid, out):
    sources = ((w0, 0), (w0, 16), (w1a, 0), (w1b, 0), (w2a, 0), (w2b, 0), (w3a, 0), (w3b, 0))
    lane = lax.broadcasted_iota(jnp.int32, (2 * TOK, 128), 1)

    def fill(i, parts):
        src, slot = tab[2 * i], tab[2 * i + 1]
        for n, (ref, at) in enumerate(sources):

            @pl.when(src == n)
            def _():
                for to, col, tile in parts:
                    which = 4 if tile is None else 2 * slot + tile
                    for t in range(16):
                        to[t * ROWS : (t + 1) * ROWS, col : col + 128] = ref[at + t, which]

        return slot

    @pl.loop(0, EXPERTS)
    def _(e):
        @pl.loop(0, 4)
        def _(b):
            fill(4 * e + b, ((wbuf, 0, 0), (wbuf, 128, 1)))
            part = jnp.dot(x_ref[b], wbuf[...], preferred_element_type=f32)

            @pl.when(b == 0)
            def _():
                acc[...] = part

            @pl.when(b > 0)
            def _():
                acc[...] += part

        first = acc[:, 0:128]
        hidden_a = (pltpu.roll(first, 64, 1) + 1.0) * first * jax.nn.sigmoid(1.702 * first)
        rest = acc[:, 128:256]
        gate = pltpu.roll(rest, 64, 1)
        hidden_b = (pltpu.roll(rest, 32, 1) + 1.0) * gate * jax.nn.sigmoid(1.702 * gate)
        hidden_a = jnp.where(lane < 64, hidden_a, 0.0).astype(bf16)
        hidden_b = jnp.where(lane < 32, hidden_b, 0.0)
        hid[e, 0, :, 0:128] = hidden_a
        hid[e, 1, :, 0:128] = hidden_a
        hid[e, 0, :, 128:256] = hidden_b.astype(bf16)
        hid[e, 1, :, 128:256] = pltpu.roll(hidden_b, 32, 1).astype(bf16)

    core = tab[32]

    @pl.loop(0, 4)
    def _(b):
        @pl.loop(0, EXPERTS)
        def _(e):
            slot = fill(4 * e + b, ((dbuf, 0, 1), (dbuf, 128, None)))
            part = lax.dot_general(
                dbuf[...], hid[e, slot], (((1,), (1,)), ((), ())), preferred_element_type=f32
            )
            part = part * mix_ref[pl.ds(e, 1), :]

            @pl.when(e == 0)
            def _():
                out[...] = part

            @pl.when(e > 0)
            def _():
                out[...] += part

        for q in range(4):
            block = out[q * 192 : (q + 1) * 192, :].astype(bf16)

            @pl.when(core == q % 2)
            def _():
                for z in range(2):
                    own_ref[8 * z + 2 * b + q // 2] = block[:, z * TOK : (z + 1) * TOK]

            @pl.when(core != q % 2)
            def _():
                for z in range(2):
                    send_ref[8 * z + 2 * b + q // 2] = block[:, z * TOK : (z + 1) * TOK]


def shards(master, moment_one, moment_two, gradient, piece_owner, tokens, routes, mix_weight):
    xi, zl, core = lax.axis_index("x"), lax.axis_index("zl"), lax.axis_index("core")
    plane = ("zl", "zh", "y", "core")

    own_x = tokens.transpose(2, 0, 1).reshape(4, 45, TOK)
    own_x = jnp.pad(own_x, ((0, 0), (0, ROWS - 45), (0, 0))).reshape(4 * ROWS, TOK)
    every_x = lax.all_gather(own_x, plane)
    x_all = every_x.reshape(2, 4, 768, TOK).transpose(1, 0, 3, 2).reshape(4, 2 * TOK, 768)

    flat_routes = routes.reshape(TOK, 2)
    flat_mix = mix_weight.reshape(TOK, 2)
    mine = jnp.sum(
        jnp.where(flat_routes[None] == jnp.arange(EXPERTS, dtype=jnp.int32)[:, None, None], flat_mix[None], 0.0), axis=2
    )
    theirs = lax.ppermute(mine, "zl", ((0, 1), (1, 0)))
    mix = jnp.where(zl == 0, jnp.concatenate([mine, theirs], 1), jnp.concatenate([theirs, mine], 1))

    inverse = jnp.zeros((16,), jnp.int32).at[piece_owner].set(jnp.arange(16, dtype=jnp.int32))
    grp = inverse // 2
    source = ((grp % 4 - xi) % 4) * 2 + grp // 4
    tab = jnp.concatenate([jnp.stack([source, inverse % 2], 1).reshape(-1), core.reshape(1)]).astype(jnp.int32)

    moment_new = beta_one * moment_one + (1.0 - beta_one) * gradient
    second_new = beta_two * moment_two + (1.0 - beta_two) * gradient * gradient
    adjust = (
        moment_new / bias_one / (jnp.sqrt(second_new / bias_two) + adam_eps) + decay_rate * master
    )
    updated = (master - learn_rate * adjust).astype(bf16)
    updated = jnp.pad(updated.transpose(0, 2, 1, 3), ((0, 0), (0, 0), (0, ROWS - 45), (0, 3072 - 2880)))

    packed = pl.pallas_call(
        pack_kernel,
        out_shape=jax.ShapeDtypeStruct((32, 5, ROWS, 128), bf16),
        compiler_params=pltpu.CompilerParams(vmem_limit_bytes=32 * 2**20),
        name="pack",
    )(updated)
    w0 = lax.all_to_all(packed, plane, 0, 0)

    up = [(i, (i + 1) % 4) for i in range(4)]
    down = [(i, (i - 1) % 4) for i in range(4)]
    w1a = lax.ppermute(w0[:16], "x", down)
    w3b = lax.ppermute(w0[16:], "x", up)
    w1b = lax.ppermute(w0[16:], "x", down)
    w3a = lax.ppermute(w0[:16], "x", up)
    w2a = lax.ppermute(w1a, "x", down)
    w2b = lax.ppermute(w3b, "x", up)

    own, send = pl.pallas_call(
        expert_kernel,
        out_shape=[jax.ShapeDtypeStruct((16, 192, TOK), bf16)] * 2,
        in_specs=[pl.BlockSpec(memory_space=pltpu.SMEM)] + [pl.BlockSpec(memory_space=pltpu.VMEM)] * 9,
        out_specs=[pl.BlockSpec(memory_space=pltpu.VMEM)] * 2,
        scratch_shapes=[
            pltpu.VMEM((768, 256), bf16),
            pltpu.VMEM((768, 256), bf16),
            pltpu.VMEM((2 * TOK, 256), f32),
            pltpu.VMEM((EXPERTS, 2, 2 * TOK, 256), bf16),
            pltpu.VMEM((768, 2 * TOK), f32),
        ],
        compiler_params=pltpu.CompilerParams(vmem_limit_bytes=56 * 2**20),
        name="experts",
    )(tab, mix, x_all, w0, w1a, w1b, w2a, w2b, w3a, w3b)

    other = lax.ppermute(send, "core", ((0, 1), (1, 0)))
    both = (own.astype(f32) + other.astype(f32)).astype(bf16)
    parts = lax.all_to_all(both, ("zl", "zh", "y"), 0, 0)
    total = jnp.sum(parts.astype(f32), axis=0).astype(bf16)
    total = total.reshape(4, ROWS, TOK)[:, :45].reshape(180, 4, 128)
    return total.transpose(1, 2, 0)


def solution(mesh):
    fine = Mesh(mesh.devices.reshape(2, 4, 2, 4, 2), ("zl", "x", "zh", "y", "core"))
    grp, tp = ("zl", "x"), ("zh", "y", "core")
    state = P(grp, tp, None, None)
    return jax.shard_map(
        shards,
        mesh=fine,
        in_specs=(state, state, state, state, P(), P(None, grp, tp), P(None, grp, None), P(None, grp, None)),
        out_specs=P(None, grp, tp),
        check_vma=False,
    )
```

time: 1030 us -> 230 us (0.22)
  the two profiles are of different devices: /device:TPU:24 before, /device:TPU:32 now
where the time goes in v1:
time: 230 us; the launch traced here: 228 us
  blocking collectives  86.5 us (38%)
  waiting for transfers between devices  52 us (23%)
  Pallas kernels  39.9 us (17%)
  local copies, waits for them, and re-layouts  14 us (6%)
  between operations  13.5 us (6%)
  other arithmetic  12.3 us (5%)
  starting transfers between devices  9.48 us (4%)
    all_to_all x1, blocking collectives, shards(): w0 = lax.all_to_all(packed, plane, 0, 0)  43.4 us
    all_to_all x1, blocking collectives, shards(): parts = lax.all_to_all(both, ('zl', 'zh', 'y'), 0, 0)  43.1 us
    pallas_call x1, Pallas kernels, shards(): pl.pallas_call(expert_kernel, out_shape=[jax.ShapeDtypeStruct((16, 192, T...  39 us
    ppermute x1, waiting for transfers between devices, shards(): w3b = lax.ppermute(w0[16:], 'x', up)  20.8 us
    ppermute x1, waiting for transfers between devices, shards(): w2b = lax.ppermute(w3b, 'x', up)  18.7 us
    transpose x1, local copies, waits for them, and re-layouts, shards(): every_x.reshape(2, 4, 768, TOK).transpose(1, 0, 3, 2)  8.64 us
    transpose x1, other arithmetic, shards(): updated.transpose(0, 2, 1, 3)  7.69 us
    ppermute x1, waiting for transfers between devices, shards(): other = lax.ppermute(send, 'core', ((0, 1), (1, 0)))  5.87 us
  transfers between devices with their start and end apart: 9, of which 6 were waited for; matrix products, arithmetic and copies ran while one was open for 9% of the time, Pallas kernels for 0%

profile of v1, /device:TPU:32, one launch (start us, length us, event | category | flops | bytes accessed | tf_op | source)
XLA Modules:
  0.0 227.7 jit_solution(12432474168518677426)
XLA Ops:
  6.5 0.0 all-gather.2.cloned.1.call-start
  6.5 1.0 reshape.25
  7.5 0.7 pad.8
  8.2 0.0 all-gather.2.cloned.1.call-update
  8.3 7.7 %fusion.8 = bf16[2,3,45,2880]{3,2,1,0:T(8,128)(2,1)S(1)} fusion(f32[2,45,3,2880]{3,0,2,1:T(2,128)} %param.10, f32[2,45,3,2880]{3,0,2,1:T(2,128)} %param.11, f32[2,45,3,2880]{3,0,2,1:T(2,128)} %param.9, f32[2,45,3,2880]{3,0,2,1:T(2,128)} %param.8), kind=kLoop, calls=%fused_computation.14 | loop fusion | flops 12441600 | bytes 13996800 | tf_op jit(solution)/shard_map/transpose | solution.py:163
  16.0 0.2 pad.9.w_ref
  16.2 0.9 pack.1
  17.1 0.0 copy-start.2
  17.1 0.0 copy-start.3
  17.1 0.0 copy-start.4
  17.1 43.4 %all_to_all.10.w0 = bf16[32,5,48,128]{3,2,1,0:T(8,128)(2,1)S(1)} all-to-all(bf16[32,5,48,128]{3,2,1,0:T(8,128)(2,1)S(1)} %pack.1), channel_id=1, replica_groups=mesh['zl'=2,'x'=4,'zh'=2,'y'=4,'core'=2] {'zl','zh','y','core'}, dimensions={0} | all-to-all | bytes 3932160 | tf_op jit(solution)/shard_map/all_to_all | solution.py:171
  60.6 0.0 copy-start
  60.6 1.9 fusion.17
  62.4 1.6 collective-permute-start.4
  64.0 1.6 collective-permute-start.1
  65.6 1.4 collective-permute-start.2
  67.1 0.6 collective-permute-start.6
  67.7 20.8 %collective-permute-done.4.w3b = bf16[16,5,48,128]{3,2,1,0:T(8,128)(2,1)S(1)} collective-permute-done((bf16[16,5,48,128]{3,2,1,0:T(8,128)(2,1)}, bf16[16,5,48,128]{3,2,1,0:T(8,128)(2,1)S(1)}, u32[]{:S(2)}, u32[]{:S(2)}) %collective-permute-start.4) | collective-permute-done | bytes 983072 | tf_op jit(solution)/shard_map/ppermute | solution.py:176
  88.5 0.0 copy-start.1
  88.5 0.4 collective-permute-start.5
  89.0 0.1 collective-permute-done.1.w1a
  89.1 2.8 %collective-permute-start.3 = (bf16[16,5,48,128]{3,2,1,0:T(8,128)(2,1)}, bf16[16,5,48,128]{3,2,1,0:T(8,128)(2,1)}, u32[]{:S(2)}, u32[]{:S(2)}) collective-permute-start(bf16[16,5,48,128]{3,2,1,0:T(8,128)(2,1)} %collective-permute-done.1.w1a), channel_id=1, source_target_pairs={{0,48},{16,0},{32,16},{48,32},{1,49},{17,1},{33,17},{49,33},{2,50}... | collective-permute-start | bytes 2949128 | tf_op jit(solution)/shard_map/ppermute | solution.py:179
  91.9 0.0 copy-done.2
  91.9 0.0 copy-done.3
  91.9 1.0 collective-permute-start
  92.9 0.0 copy-done.4
  92.9 0.6 scatter_custom_fusion
  93.5 0.1 copy.43
  93.6 0.1 reshape.23
  93.7 0.6 pad_add_fusion.1.tab
  94.3 1.3 collective-permute-done
  95.6 0.6 maximum_select_fusion.mix_ref
  96.2 0.0 all-gather.2.cloned.1.call-done
  96.2 8.6 %copy.46 = bf16[4,2,512,768]{3,2,1,0:T(8,128)(2,1)} copy(bf16[4,2,512,768]{2,3,0,1:T(8,128)(2,1)} %bitcast.20) | data formatting | bytes 12582912 | tf_op jit(solution)/shard_map/transpose | solution.py:142
  104.9 0.0 copy-done
  104.9 0.0 copy-done.1
  104.9 5.2 %collective-permute-done.2.w1b = bf16[16,5,48,128]{3,2,1,0:T(8,128)(2,1)} collective-permute-done((bf16[16,5,48,128]{3,2,1,0:T(8,128)(2,1)}, bf16[16,5,48,128]{3,2,1,0:T(8,128)(2,1)}, u32[]{:S(2)}, u32[]{:S(2)}) %collective-permute-start.2) | collective-permute-done | bytes 983072 | tf_op jit(solution)/shard_map/ppermute | solution.py:177
  110.1 0.0 collective-permute-done.6.w3a
  110.1 18.7 %collective-permute-done.5.w2b = bf16[16,5,48,128]{3,2,1,0:T(8,128)(2,1)} collective-permute-done((bf16[16,5,48,128]{3,2,1,0:T(8,128)(2,1)S(1)}, bf16[16,5,48,128]{3,2,1,0:T(8,128)(2,1)}, u32[]{:S(2)}, u32[]{:S(2)}) %collective-permute-start.5) | collective-permute-done | bytes 983072 | tf_op jit(solution)/shard_map/ppermute | solution.py:180
  128.8 0.0 collective-permute-done.3.w2a
  128.8 39.0 %experts.1 = (bf16[16,192,512]{2,1,0:T(8,128)(2,1)}, bf16[16,192,512]{2,1,0:T(8,128)(2,1)}) custom-call(s32[33]{0:T(128)} %pad_add_fusion.1.tab, f32[4,1024]{1,0:T(4,128)} %maximum_select_fusion.mix_ref, bf16[4,1024,768]{2,1,0:T(8,128)(2,1)} %bitcast.19, bf16[32,5,48,128]{3,2,1,0:T(8,128)(2,1)} %copy-done, ...), custom_call_target="tpu_custom_call" | custom-call | tf_op jit(solution)/shard_map/experts/pallas_call | solution.py:182
  167.8 0.0 collective-permute-start.7
  167.8 5.9 %collective-permute-done.7 = bf16[16,192,512]{2,1,0:T(8,128)(2,1)S(1)} collective-permute-done((bf16[16,192,512]{2,1,0:T(8,128)(2,1)}, bf16[16,192,512]{2,1,0:T(8,128)(2,1)S(1)}, u32[]{:S(2)}, u32[]{:S(2)}) %collective-permute-start.7) | collective-permute-done | bytes 3145760 | tf_op jit(solution)/shard_map/ppermute | solution.py:198
  173.7 2.9 %add_convert_fusion = bf16[16,192,512]{2,1,0:T(8,128)(2,1)S(1)} fusion(bf16[16,192,512]{2,1,0:T(8,128)(2,1)S(1)} %collective-permute-done.7, bf16[16,192,512]{2,1,0:T(8,128)(2,1)} %get-tuple-element.7), kind=kLoop, calls=%fused_computation.1 | loop fusion | flops 6291456 | bytes 9437184 | tf_op jit(solution)/shard_map/convert_element_type | solution.py:199
  176.6 43.1 %all_to_all.11 = bf16[16,192,512]{2,1,0:T(8,128)(2,1)S(1)} all-to-all(bf16[16,192,512]{2,1,0:T(8,128)(2,1)S(1)} %add_convert_fusion), channel_id=1, replica_groups=mesh['zl'=2,'x'=4,'zh'=2,'y'=4,'core'=2] {'zl','zh','y'}, dimensions={0} | all-to-all | bytes 6291456 | tf_op jit(solution)/shard_map/all_to_all | solution.py:200
  219.7 0.5 reduce_sum.22
  220.1 0.7 reshape.29
  (5 shorter events, 0.1 us)
Async XLA Ops:
  6.5 89.7 %all-gather.2.cloned.1.call-start = ((), (), s32[]{:S(2)}) async-start(), calls=%async_computation.2 | async-start | bytes 6488064 | tf_op jit(solution)/shard_map/all_gather | solution.py:141
  17.1 74.8 %copy-start.2 = (f32[4,128,2]{1,2,0:T(2,128)S(1)}, f32[4,128,2]{1,2,0:T(2,128)}, u32[]{:S(2)}) copy-start(f32[4,128,2]{1,2,0:T(2,128)} %param.15) | copy-start | bytes 12292
  17.1 74.7 %copy-start.3 = (s32[4,128,2]{1,2,0:T(2,128)S(1)}, s32[4,128,2]{1,2,0:T(2,128)}, u32[]{:S(2)}) copy-start(s32[4,128,2]{1,2,0:T(2,128)} %param.14) | copy-start | bytes 12292
  17.1 75.7 %copy-start.4 = (s32[16]{0:T(128)S(1)}, s32[16]{0:T(128)}, u32[]{:S(2)}) copy-start(s32[16]{0:T(128)} %param.12) | copy-start | bytes 196
  60.6 44.3 %copy-start = (bf16[32,5,48,128]{3,2,1,0:T(8,128)(2,1)}, bf16[32,5,48,128]{3,2,1,0:T(8,128)(2,1)S(1)}, u32[]{:S(2)}) copy-start(bf16[32,5,48,128]{3,2,1,0:T(8,128)(2,1)S(1)} %all_to_all.10.w0) | copy-start | bytes 5898244
  62.4 26.1 %collective-permute-start.4 = (bf16[16,5,48,128]{3,2,1,0:T(8,128)(2,1)}, bf16[16,5,48,128]{3,2,1,0:T(8,128)(2,1)S(1)}, u32[]{:S(2)}, u32[]{:S(2)}) collective-permute-start(bf16[16,5,48,128]{3,2,1,0:T(8,128)(2,1)} %get-tuple-element.9), channel_id=1, source_target_pairs={{0,16},{16,32},{32,48},{48,0},{1,17},{17,33},{33,49},{49,1},{2,18}... | collective-permute-start | bytes 2949128 | tf_op jit(solution)/shard_map/ppermute | solution.py:176
  64.0 25.0 %collective-permute-start.1 = (bf16[16,5,48,128]{3,2,1,0:T(8,128)(2,1)}, bf16[16,5,48,128]{3,2,1,0:T(8,128)(2,1)}, u32[]{:S(2)}, u32[]{:S(2)}) collective-permute-start(bf16[16,5,48,128]{3,2,1,0:T(8,128)(2,1)} %get-tuple-element.10), channel_id=1, source_target_pairs={{0,48},{16,0},{32,16},{48,32},{1,49},{17,1},{33,17},{49,33},{2,50}... | collective-permute-start | bytes 2949128 | tf_op jit(solution)/shard_map/ppermute | solution.py:175
  65.6 44.5 %collective-permute-start.2 = (bf16[16,5,48,128]{3,2,1,0:T(8,128)(2,1)}, bf16[16,5,48,128]{3,2,1,0:T(8,128)(2,1)}, u32[]{:S(2)}, u32[]{:S(2)}) collective-permute-start(bf16[16,5,48,128]{3,2,1,0:T(8,128)(2,1)} %get-tuple-element.9), channel_id=1, source_target_pairs={{0,48},{16,0},{32,16},{48,32},{1,49},{17,1},{33,17},{49,33},{2,50}... | collective-permute-start | bytes 2949128 | tf_op jit(solution)/shard_map/ppermute | solution.py:177
  67.1 43.0 %collective-permute-start.6 = (bf16[16,5,48,128]{3,2,1,0:T(8,128)(2,1)}, bf16[16,5,48,128]{3,2,1,0:T(8,128)(2,1)}, u32[]{:S(2)}, u32[]{:S(2)}) collective-permute-start(bf16[16,5,48,128]{3,2,1,0:T(8,128)(2,1)} %get-tuple-element.10), channel_id=1, source_target_pairs={{0,16},{16,32},{32,48},{48,0},{1,17},{17,33},{33,49},{49,1},{2,18}... | collective-permute-start | bytes 2949128 | tf_op jit(solution)/shard_map/ppermute | solution.py:178
  88.5 16.4 %copy-start.1 = (bf16[16,5,48,128]{3,2,1,0:T(8,128)(2,1)}, bf16[16,5,48,128]{3,2,1,0:T(8,128)(2,1)S(1)}, u32[]{:S(2)}) copy-start(bf16[16,5,48,128]{3,2,1,0:T(8,128)(2,1)S(1)} %collective-permute-done.4.w3b) | copy-start | bytes 2949124
  88.5 40.3 %collective-permute-start.5 = (bf16[16,5,48,128]{3,2,1,0:T(8,128)(2,1)S(1)}, bf16[16,5,48,128]{3,2,1,0:T(8,128)(2,1)}, u32[]{:S(2)}, u32[]{:S(2)}) collective-permute-start(bf16[16,5,48,128]{3,2,1,0:T(8,128)(2,1)S(1)} %collective-permute-done.4.w3b), channel_id=1, source_target_pairs={{0,16},{16,32},{32,48},{48,0},{1,17},{17,33},{33,49},{49,1},{2,18}... | collective-permute-start | bytes 2949128 | tf_op jit(solution)/shard_map/ppermute | solution.py:180
  89.1 39.7 %collective-permute-start.3 = (bf16[16,5,48,128]{3,2,1,0:T(8,128)(2,1)}, bf16[16,5,48,128]{3,2,1,0:T(8,128)(2,1)}, u32[]{:S(2)}, u32[]{:S(2)}) collective-permute-start(bf16[16,5,48,128]{3,2,1,0:T(8,128)(2,1)} %collective-permute-done.1.w1a), channel_id=1, source_target_pairs={{0,48},{16,0},{32,16},{48,32},{1,49},{17,1},{33,17},{49,33},{2,50}... | collective-permute-start | bytes 2949128 | tf_op jit(solution)/shard_map/ppermute | solution.py:179
  91.9 3.7 %collective-permute-start = (f32[4,512]{1,0:T(4,128)S(1)}, f32[4,512]{1,0:T(4,128)S(1)}, u32[]{:S(2)}, u32[]{:S(2)}) collective-permute-start(f32[4,512]{1,0:T(4,128)S(1)} %select_reduce_fusion), channel_id=1, source_target_pairs={{0,64},{64,0},{1,65},{65,1},{2,66},{66,2},{3,67},{67,3},{4,68},{68... | collective-permute-start | bytes 24584 | tf_op jit(solution)/shard_map/ppermute | solution.py:149
  167.8 5.9 %collective-permute-start.7 = (bf16[16,192,512]{2,1,0:T(8,128)(2,1)}, bf16[16,192,512]{2,1,0:T(8,128)(2,1)S(1)}, u32[]{:S(2)}, u32[]{:S(2)}) collective-permute-start(bf16[16,192,512]{2,1,0:T(8,128)(2,1)} %get-tuple-element.8), channel_id=1, source_target_pairs={{0,1},{1,0},{2,3},{3,2},{4,5},{5,4},{6,7},{7,6},{8,9},{9,8},{10,11... | collective-permute-start | bytes 9437192 | tf_op jit(solution)/shard_map/ppermute | solution.py:198
Sparse Core Ops, SparseCore 0:
  9.1 82.7 all-gather.1

commit v2 on v0

v2 whole, which is shorter than its diff:
```python
import functools

import jax
import jax.numpy as jnp
from jax import lax
from jax.experimental import pallas as pl
from jax.experimental.pallas import tpu as pltpu
from jax.sharding import Mesh
from jax.sharding import PartitionSpec as P

EXPERTS = 4
ROWS = 48
PART = 56
TOK = 512
HALF = 1536

learn_rate = 0.003
beta_one = 0.9
beta_two = 0.999
adam_eps = 1e-08
decay_rate = 0.1
bias_one = 1.0 - 0.9**20
bias_two = 1.0 - 0.999**20

bf16 = jnp.bfloat16
f32 = jnp.float32


def roll(x, by):
    if isinstance(by, int):
        by = by % 128
        if by == 0:
            return x
    return pltpu.roll(x, by, 1)


def pack_kernel(place, w_ref, o_ref):
    xl, zl = place[0], place[1]
    lane = lax.broadcasted_iota(jnp.int32, (ROWS, 128), 1)
    lane8 = lax.broadcasted_iota(jnp.int32, (8, 128), 1)
    within = lane % 64

    @pl.loop(0, 8)
    def _(k):
        def tile(s, kind, j):
            return w_ref[s, kind, :, pl.ds(pl.multiple_of(k * 384 + j * 128, 128), 128)].astype(f32)

        for i in range(16):
            a, off = (24 * i) // 128, (24 * i) % 128

            def source(s, kind):
                if off <= 104:
                    return tile(s, kind, a)
                return jnp.where(lane >= off, tile(s, kind, a), tile(s, kind, a + 1))

            pair = 2 * k + i // 8
            link_x, link_z = pair // 4, pair % 4
            jx, jz = (link_x + xl) % 2, (link_z + zl) % 2
            x_to, z_to = (link_x + jx) % 4, (link_z + jz) % 4
            to = (x_to // 2) * 16 + (z_to // 2) * 8 + i % 8
            halves, fold = [], jnp.zeros((8, 128), f32)
            for s in range(2):
                gate, up, down = source(s, 0), source(s, 1), source(s, 2)
                half = 64 * ((s + i // 8) % 2)
                gate, up = roll(gate, half - off), roll(up, half + 24 - off)
                main_down = roll(down, half + 48 - off)
                halves.append(jnp.where(within < 24, gate, jnp.where(within < 48, up, main_down)))
                for g in range(6):
                    at = 16 * g + 8 * s
                    rest = roll(down[8 * g : 8 * g + 8], at - off - 16)
                    fold = jnp.where((lane8 >= at) & (lane8 < at + 8), rest, fold)
            main = jnp.where(lane < 64, halves[i // 8], halves[1 - i // 8])
            o_ref[to, 2 * jx + jz] = jnp.concatenate([main, fold], 0).astype(bf16)


def assemble_kernel(along_x, place, *refs):
    *parts, o_ref = refs
    if len(parts) == 1:
        part = [lambda src, m=m: parts[0][src, m] for m in range(4)]
    elif along_x:
        part = [lambda src, m=m: parts[m // 2][m % 2, src] for m in range(4)]
    else:
        part = [lambda src, m=m: parts[m % 2][m // 2, src] for m in range(4)]
    lane = lax.broadcasted_iota(jnp.int32, (ROWS, 128), 1)
    lane8 = lax.broadcasted_iota(jnp.int32, (8, 128), 1)

    for zl in range(2):

        @pl.when(place[1] == zl)
        def _():
            @pl.loop(0, 32)
            def _(src):
                row = pl.ds(pl.multiple_of((src % 16) * ROWS, ROWS), ROWS)
                loaded = [part[m](src).astype(f32) for m in range(4)]
                for slot in range(2):
                    swap = slot ^ zl
                    for pair in range(2):
                        first, second = loaded[2 * pair], loaded[2 * pair + 1]
                        main = roll(jnp.where((lane // 64) == swap, first[:ROWS], second[:ROWS]), swap * 64)
                        rows = []
                        for g in range(6):
                            at = 16 * g + 8 * slot
                            low, high = roll(second[ROWS:], -at), roll(first[ROWS:], 64 - at)
                            cur = main[8 * g : 8 * g + 8]
                            rows.append(jnp.where(lane8 < 8, low, jnp.where((lane8 // 8) == 8, high, cur)))
                        col = slice(pair * 128, pair * 128 + 128)
                        piece = (src // 16) * 2 + slot
                        o_ref[0, piece, row, col] = main.astype(bf16)
                        o_ref[1, piece, row, col] = jnp.concatenate(rows, 0).astype(bf16)


def expert_kernel(tab, mix_ref, *refs):
    xs, ws, (own_ref, send_ref) = refs[:4], refs[4:8], refs[8:10]
    x, wg, wd, hid, stage, xsem, gsem, dsem, osem = refs[10:]
    core, y = tab[32], tab[33]

    gets = []
    for side in range(2):
        near, rest = xs[2 * side : 2 * side + 2]
        for at in range(4):
            ref = (near, rest)[at // 2].at[pl.ds(at % 2 * 2 * TOK, 2 * TOK)]
            to = x.at[:, pl.ds(side * HALF + at * 384, 384)]
            gets.append(pltpu.make_async_copy(ref, to, xsem.at[len(gets)]))
            gets[-1].start()

    def fetch(use):
        @pl.loop(0, 16)
        def _(i):
            e, b = i // 4, i % 4
            src, slot = tab[2 * i], tab[2 * i + 1]
            piece = (src % 2) * 2 + slot
            for relation in range(4):

                @pl.when(src // 2 == relation)
                def _():
                    for q in range(4):
                        away_y = (2 * (b % 2) + q // 2 + 4 - y) % 4
                        side = (q + core) % 2
                        row = pl.multiple_of(side * HALF + away_y * 384 + (b // 2) * 192, 192)
                        block = ws[relation].at[use, piece, pl.ds(192 * q, 192)]
                        if use == 0:
                            pltpu.make_async_copy(block, wg.at[e, pl.ds(row, 192)], gsem.at[e]).start()
                        else:
                            to = wd.at[pl.ds(row, 192), pl.ds(pl.multiple_of(e * 256, 256), 256)]
                            pltpu.make_async_copy(block, to, dsem).start()

    fetch(0)
    fetch(1)
    for get in gets:
        get.wait()

    lanes = lax.broadcasted_iota(jnp.int32, (2 * TOK, 128), 1) % 64

    @pl.loop(0, EXPERTS)
    def _(e):
        pltpu.make_async_copy(wg.at[e], wg.at[e], gsem.at[e]).wait()
        acc = jnp.dot(x[...], wg[e], preferred_element_type=f32)
        mix = mix_ref[e]
        for n in range(2):
            gate = acc[:, n * 128 : (n + 1) * 128]
            hidden = (pltpu.roll(gate, 104, 1) + 1.0) * gate * jax.nn.sigmoid(1.702 * gate)
            hidden = hidden.astype(bf16).astype(f32) * mix
            hidden = jnp.where((lanes >= 48) | (lanes < 8), pltpu.roll(hidden, 48, 1), 0.0)
            hid[:, pl.ds(pl.multiple_of(e * 256 + n * 128, 128), 128)] = hidden.astype(bf16)

    pltpu.make_async_copy(wd, wd, dsem).wait()

    def put_wait(slot):
        pltpu.make_async_copy(stage.at[slot], stage.at[slot], osem.at[slot]).wait()

    @pl.loop(0, 4)
    def _(k):
        side, n, slot = 1 - k // 2, k % 2, k % 2
        rows = pl.ds(pl.multiple_of(side * HALF + n * 768, 768), 768)
        out = lax.dot_general(wd[rows, :], hid[...], (((1,), (1,)), ((), ())), preferred_element_type=f32)

        @pl.when(k >= 2)
        def _():
            put_wait(slot)

        stage[slot] = out.astype(bf16)
        for ref, want in ((own_ref, 0), (send_ref, 1)):

            @pl.when(side == want)
            def _():
                for q in range(4):
                    for z in range(2):
                        at = 8 * z + 4 * (q % 2) + (2 * n + q // 2 + y) % 4
                        block = stage.at[slot, pl.ds(q * 192, 192), pl.ds(z * TOK, TOK)]
                        pltpu.make_async_copy(block, ref.at[at], osem.at[slot]).start()

    put_wait(0)
    put_wait(1)


def shards(master, moment_one, moment_two, gradient, piece_owner, tokens, routes, mix_weight):
    xl, zl, core = lax.axis_index("xl"), lax.axis_index("zl"), lax.axis_index("core")
    chips = ("xh", "zh", "y")
    swap = ((0, 1), (1, 0))
    plus = [(i, (i + 1) % 4) for i in range(4)]
    minus = [(i, (i - 1) % 4) for i in range(4)]

    own_x = tokens.transpose(2, 0, 1).reshape(4, 45, TOK)
    own_x = jnp.pad(own_x, ((0, 0), (0, ROWS - 45), (0, 0))).reshape(4 * ROWS, TOK)
    xh, zh = lax.axis_index("xh"), lax.axis_index("zh")
    at_z, at_x = lax.ppermute(own_x, "zh", swap), lax.ppermute(own_x, "xh", swap)
    at_xz = lax.ppermute(own_x, ("xh", "zh"), ((0, 3), (1, 2), (2, 1), (3, 0)))

    def in_order(first, here, other):
        return jnp.stack([jnp.where(first, here, other), jnp.where(first, other, here)])

    swapped = own_x, at_z, at_x, at_xz

    flat_routes = routes.reshape(TOK, 2)
    flat_mix = mix_weight.reshape(TOK, 2)
    mine = jnp.sum(
        jnp.where(flat_routes[None] == jnp.arange(EXPERTS, dtype=jnp.int32)[:, None, None], flat_mix[None], 0.0), axis=2
    )
    theirs = lax.ppermute(mine, "xh", swap)
    mix = jnp.where(
        xh == 0, jnp.concatenate([mine, theirs], 1), jnp.concatenate([theirs, mine], 1)
    )

    inverse = jnp.zeros((16,), jnp.int32).at[piece_owner].set(jnp.arange(16, dtype=jnp.int32))
    grp = inverse // 2
    relation = ((grp % 2) ^ xl) * 2 + ((grp // 4) ^ zl)
    source = relation * 2 + (grp % 4) // 2
    tab = jnp.concatenate([jnp.stack([source, inverse % 2], 1).reshape(-1), jnp.stack([core, lax.axis_index("y")])]).astype(jnp.int32)
    place = jnp.stack([xl, zl]).astype(jnp.int32)

    moment_new = beta_one * moment_one + (1.0 - beta_one) * gradient
    second_new = beta_two * moment_two + (1.0 - beta_two) * gradient * gradient
    adjust = (
        moment_new / bias_one / (jnp.sqrt(second_new / bias_two) + adam_eps) + decay_rate * master
    )
    updated = (master - learn_rate * adjust).astype(bf16)
    updated = jnp.pad(updated.transpose(0, 2, 1, 3), ((0, 0), (0, 0), (0, ROWS - 45), (0, 3072 - 2880)))

    smem, vmem = pl.BlockSpec(memory_space=pltpu.SMEM), pl.BlockSpec(memory_space=pltpu.VMEM)
    packed = pl.pallas_call(
        pack_kernel,
        out_shape=jax.ShapeDtypeStruct((32, 4, PART, 128), bf16),
        in_specs=[smem, vmem],
        out_specs=vmem,
        compiler_params=pltpu.CompilerParams(vmem_limit_bytes=32 * 2**20),
        name="pack",
    )(place, updated)
    packed, swapped, mix = lax.optimization_barrier((packed, swapped, mix))
    w0 = lax.all_to_all(packed, ("xh", "zh", "y", "core"), 0, 0)
    held = in_order(xh == 0, in_order(zh == 0, *swapped[:2]), in_order(zh == 0, *swapped[2:]))
    held = held.transpose(0, 3, 1, 2).reshape(2 * TOK, 384)
    held, w0 = lax.optimization_barrier((held, w0))

    ax, az = ("xh", "xl"), ("zl", "zh")
    plus_z = [((i % 2) * 2 + i // 2, (j % 2) * 2 + j // 2) for i, j in plus]
    minus_z = [(j, i) for i, j in plus_z]

    def along_x(block, i):
        return lax.ppermute(block, ax, plus if i else minus)

    def along_z(block, j):
        return lax.ppermute(block, az, plus_z if j else minus_z)

    grid = w0.reshape(32, 2, 2, PART, 128)
    from_x = [along_x(jnp.swapaxes(grid[:, 1 - i], 0, 1), i) for i in range(2)]
    from_z = [along_z(jnp.swapaxes(grid[:, :, 1 - j], 0, 1), j) for j in range(2)]

    def assemble(parts, name):
        return pl.pallas_call(
            functools.partial(assemble_kernel, name != "pieces_z"),
            out_shape=jax.ShapeDtypeStruct((2, 4, 768, 256), bf16),
            in_specs=[smem] + [vmem] * len(parts),
            out_specs=vmem,
            compiler_params=pltpu.CompilerParams(vmem_limit_bytes=32 * 2**20),
            cost_estimate=pl.CostEstimate(flops=0, bytes_accessed=16 * 2**20, transcendentals=0),
            name=name,
        )(place, *parts)

    above = lax.ppermute(held, "y", minus)
    mix = jnp.broadcast_to(mix[:, :, None], (EXPERTS, 2 * TOK, 128))
    place, mix = lax.optimization_barrier((place, mix))
    here = assemble([w0], "pieces_here")
    above, from_x, from_z, here = lax.optimization_barrier((above, from_x, from_z, here))

    diagonal = [along_x(jnp.stack([from_z[0][1 - i], from_z[1][1 - i]]), i) for i in range(2)]
    below, far = lax.ppermute(held, "y", plus), lax.ppermute(above, "y", minus)
    near = jnp.concatenate([held, above], 0)
    x_near = lax.ppermute(near, "core", swap)
    ws = [here, assemble(from_z, "pieces_z"), assemble(from_x, "pieces_x")]
    diagonal, below, far, x_near, ws = lax.optimization_barrier((diagonal, below, far, x_near, ws))
    rest = jnp.concatenate([far, below], 0)
    x_rest = lax.ppermute(rest, "core", swap)
    ws.append(assemble(diagonal, "pieces_diagonal"))
    xs = [near, rest, x_near, x_rest]

    hbm = pl.BlockSpec(memory_space=pl.ANY)
    own_sum, send = pl.pallas_call(
        expert_kernel,
        out_shape=[jax.ShapeDtypeStruct((16, 192, TOK), bf16)] * 2,
        in_specs=[smem, vmem] + [hbm] * 8,
        out_specs=[hbm] * 2,
        scratch_shapes=[
            pltpu.VMEM((2 * TOK, 2 * HALF), bf16),
            pltpu.VMEM((EXPERTS, 2 * HALF, 256), bf16),
            pltpu.VMEM((2 * HALF, EXPERTS * 256), bf16),
            pltpu.VMEM((2 * TOK, EXPERTS * 256), bf16),
            pltpu.VMEM((2, 768, 2 * TOK), bf16),
            pltpu.SemaphoreType.DMA((8,)),
            pltpu.SemaphoreType.DMA((EXPERTS,)),
            pltpu.SemaphoreType.DMA,
            pltpu.SemaphoreType.DMA((2,)),
        ],
        compiler_params=pltpu.CompilerParams(vmem_limit_bytes=58 * 2**20),
        name="experts",
    )(tab, mix, *xs, *ws)

    other = lax.ppermute(send, "core", swap)
    both = (own_sum.astype(f32) + other.astype(f32)).astype(bf16)
    parts = lax.all_to_all(both, chips, 0, 0)
    total = jnp.sum(parts.astype(f32), axis=0).astype(bf16)
    total = total.reshape(4, ROWS, TOK)[:, :45].reshape(180, 4, 128)
    return total.transpose(1, 2, 0)


def solution(mesh):
    fine = Mesh(mesh.devices.reshape(2, 2, 2, 2, 4, 2), ("zl", "xh", "xl", "zh", "y", "core"))
    grp, tp = ("zl", "xh", "xl"), ("zh", "y", "core")
    state = P(grp, tp, None, None)
    return jax.shard_map(
        shards,
        mesh=fine,
        in_specs=(state, state, state, state, P(), P(None, grp, tp), P(None, grp, None), P(None, grp, None)),
        out_specs=P(None, grp, tp),
        check_vma=False,
    )
```

time: 1030 us -> 207 us (0.20)
  the two profiles are of different devices: /device:TPU:24 before, /device:TPU:32 now
where the time goes in v2:
time: 207 us
  waiting for transfers between devices  50.5 us (24%)
  blocking collectives  47.9 us (23%)
  Pallas kernels  44 us (21%)
  starting transfers between devices  27.6 us (13%)
  local copies, waits for them, and re-layouts  21.8 us (11%)
  other arithmetic  14.8 us (7%)
    all_to_all x1, blocking collectives, shards(): parts = lax.all_to_all(both, chips, 0, 0)  47.9 us
    all_to_all x1, waiting for transfers between devices, shards(): w0 = lax.all_to_all(packed, ('xh', 'zh', 'y', 'core'), 0, 0)  25 us
    pallas_call x1, Pallas kernels, shards(): pl.pallas_call(expert_kernel, out_shape=[jax.ShapeDtypeStruct((16, 192, T...  22.6 us
    pallas_call x4, Pallas kernels, assemble(): pl.pallas_call(functools.partial(assemble_kernel, name != 'pieces_z'), ou...  17.1 us
    ppermute x1, waiting for transfers between devices, shards(): above = lax.ppermute(held, 'y', minus)  11.8 us
    unnamed x26, local copies, waits for them, and re-layouts  11.6 us
    transpose x1, other arithmetic, shards(): updated.transpose(0, 2, 1, 3)  7.67 us
    all_to_all x1, starting transfers between devices, shards(): w0 = lax.all_to_all(packed, ('xh', 'zh', 'y', 'core'), 0, 0)  7.29 us
  transfers between devices with their start and end apart: 17, of which 7 were waited for; matrix products, arithmetic and copies ran while one was open for 10% of the time, Pallas kernels for 10%

profile of v2, /device:TPU:32, one launch (start us, length us, event | category | flops | bytes accessed | tf_op | source)
XLA Modules:
  0.0 207.0 jit_solution(437461964239233545)
XLA Ops:
  0.0 1.0 reshape.143
  1.0 0.7 pad.9
  1.7 5.4 %collective-permute-start.2 = (bf16[192,512]{1,0:T(8,128)(2,1)}, bf16[192,512]{1,0:T(8,128)(2,1)}, u32[]{:S(2)}, u32[]{:S(2)}) collective-permute-start(bf16[192,512]{1,0:T(8,128)(2,1)} %bitcast.8), channel_id=1, source_target_pairs={{0,40},{8,32},{32,8},{40,0},{1,41},{9,33},{33,9},{41,1},{2,42},{10... | collective-permute-start | bytes 589832 | tf_op jit(solution)/shard_map/ppermute | solution.py:207
  8.2 0.7 select_reduce_fusion
  8.9 3.1 %collective-permute-start.3 = (f32[4,512]{1,0:T(4,128)S(1)}, f32[4,512]{1,0:T(4,128)S(1)}, u32[]{:S(2)}, u32[]{:S(2)}) collective-permute-start(f32[4,512]{1,0:T(4,128)S(1)} %select_reduce_fusion), channel_id=1, source_target_pairs={{0,32},{32,0},{1,33},{33,1},{2,34},{34,2},{3,35},{35,3},{4,36},{36... | collective-permute-start | bytes 24584 | tf_op jit(solution)/shard_map/ppermute | solution.py:219
  12.0 7.7 %fusion.8 = bf16[2,3,45,2880]{3,2,1,0:T(8,128)(2,1)S(1)} fusion(f32[2,45,3,2880]{3,0,2,1:T(2,128)} %param.10, f32[2,45,3,2880]{3,0,2,1:T(2,128)} %param.11, f32[2,45,3,2880]{3,0,2,1:T(2,128)} %param.9, f32[2,45,3,2880]{3,0,2,1:T(2,128)} %param.8), kind=kLoop, calls=%fused_computation.14 | loop fusion | flops 12441600 | bytes 13996800 | tf_op jit(solution)/shard_map/transpose | solution.py:237
  20.0 4.3 %pack.1 = bf16[32,4,56,128]{3,2,1,0:T(8,128)(2,1)S(1)} custom-call(s32[2]{0:T(128)S(1)} %pad_add_fusion.2.place, bf16[2,3,48,3072]{3,2,1,0:T(8,128)(2,1)S(1)} %pad.8.w_ref), custom_call_target="tpu_custom_call" | custom-call | tf_op jit(solution)/shard_map/pack/pallas_call | solution.py:240
  24.3 1.2 copy-done.4
  25.6 0.6 maximum_select_fusion
  26.2 7.3 %all-to-all-start = ((bf16[32,4,56,128]{3,2,1,0:T(8,128)(2,1)}), bf16[32,4,56,128]{3,2,1,0:T(8,128)(2,1)S(1)}, u32[]{:S(2)}, u32[]{:S(2)}) async-start(bf16[32,4,56,128]{3,2,1,0:T(8,128)(2,1)} %copy-done.4), calls=%async_computation | async-start | bytes 3670016 | tf_op jit(solution)/shard_map/all_to_all | solution.py:249
  33.5 1.3 select_bitcast_fusion.1
  35.0 0.8 copy.51
  35.9 25.0 %all-to-all-done.refs_0_ = bf16[32,4,56,128]{3,2,1,0:T(8,128)(2,1)S(1)} async-done(((bf16[32,4,56,128]{3,2,1,0:T(8,128)(2,1)}), bf16[32,4,56,128]{3,2,1,0:T(8,128)(2,1)S(1)}, u32[]{:S(2)}, u32[]{:S(2)}) %all-to-all-start) | async-done | bytes 1835040 | tf_op jit(solution)/shard_map/all_to_all | solution.py:249
  61.2 1.0 copy.92
  62.2 1.1 copy.93
  63.3 1.0 collective-permute-start.7
  64.3 1.0 collective-permute-start.8
  65.3 1.0 copy.94
  66.3 1.0 copy.95
  67.3 1.3 collective-permute-start.5
  68.6 0.8 collective-permute-start.6
  69.4 1.2 copy.57
  70.5 0.6 collective-permute-start.4
  71.1 2.6 %broadcast_in_dim.28.mix_ref = f32[4,1024,128]{2,1,0:T(8,128)} broadcast(f32[4,1024]{1,0:T(4,128)} %maximum_select_fusion), dimensions={0,1} | broadcast | bytes 2113536 | tf_op jit(solution)/shard_map/broadcast_in_dim | solution.py:280
  73.8 3.8 %pieces_here.1.refs_4_ = bf16[2,4,768,256]{3,2,1,0:T(8,128)(2,1)S(1)} custom-call(s32[2]{0:T(128)S(1)} %pad_add_fusion.2.place, bf16[32,4,56,128]{3,2,1,0:T(8,128)(2,1)S(1)} %all-to-all-done.refs_0_), custom_call_target="tpu_custom_call" | custom-call | bytes 16777216 | tf_op jit(solution)/shard_map/pieces_here/pallas_call | solution.py:269
  77.6 11.8 %collective-permute-done.4 = bf16[1024,384]{1,0:T(8,128)(2,1)S(1)} collective-permute-done((bf16[1024,384]{1,0:T(8,128)(2,1)}, bf16[1024,384]{1,0:T(8,128)(2,1)S(1)}, u32[]{:S(2)}, u32[]{:S(2)}) %collective-permute-start.4) | collective-permute-done | bytes 786464 | tf_op jit(solution)/shard_map/ppermute | solution.py:279
  89.7 2.5 %collective-permute-done.6.refs_1_ = bf16[2,32,56,128]{3,2,1,0:T(8,128)(2,1)} collective-permute-done((bf16[2,32,56,128]{3,2,1,0:T(8,128)(2,1)}, bf16[2,32,56,128]{3,2,1,0:T(8,128)(2,1)}, u32[]{:S(2)}, u32[]{:S(2)}) %collective-permute-start.6) | collective-permute-done | bytes 917536 | tf_op jit(solution)/shard_map/ppermute | solution.py:259
  92.5 1.6 fusion.15
  94.7 1.8 collective-permute-start.10
  96.5 1.2 collective-permute-start.11
  97.7 2.0 collective-permute-start.12
  99.7 4.5 %pieces_z.1.refs_5_ = bf16[2,4,768,256]{3,2,1,0:T(8,128)(2,1)S(1)} custom-call(s32[2]{0:T(128)S(1)} %pad_add_fusion.2.place, bf16[2,32,56,128]{3,2,1,0:T(8,128)(2,1)S(1)} %collective-permute-done.7.refs_0_, bf16[2,32,56,128]{3,2,1,0:T(8,128)(2,1)} %collective-permute-done.8.refs_1_), custom_call_target="tpu_custom_call" | custom-call | bytes 16777216 | tf_op jit(solution)/shard_map/pieces_z/pallas_call | solution.py:269
  104.3 1.7 copy-done.1
  105.9 5.0 %pieces_x.1.refs_6_ = bf16[2,4,768,256]{3,2,1,0:T(8,128)(2,1)S(1)} custom-call(s32[2]{0:T(128)S(1)} %pad_add_fusion.2.place, bf16[2,32,56,128]{3,2,1,0:T(8,128)(2,1)} %collective-permute-done.5.refs_0_, bf16[2,32,56,128]{3,2,1,0:T(8,128)(2,1)} %collective-permute-done.6.refs_1_), custom_call_target="tpu_custom_call" | custom-call | bytes 16777216 | tf_op jit(solution)/shard_map/pieces_x/pallas_call | solution.py:269
  110.9 1.7 copy-done.2
  112.6 4.1 %collective-permute-done.11 = bf16[1024,384]{1,0:T(8,128)(2,1)S(1)} collective-permute-done((bf16[1024,384]{1,0:T(8,128)(2,1)S(1)}, bf16[1024,384]{1,0:T(8,128)(2,1)S(1)}, u32[]{:S(2)}, u32[]{:S(2)}) %collective-permute-start.11) | collective-permute-done | bytes 786464 | tf_op jit(solution)/shard_map/ppermute | solution.py:286
  116.7 1.4 collective-permute-done.10.refs_1_
  118.3 1.0 copy-done.8
  119.3 0.6 scatter_custom_fusion
  120.2 0.6 pad_add_fusion.1.tab
  120.8 3.9 %pieces_diagonal.1.refs_7_ = bf16[2,4,768,256]{3,2,1,0:T(8,128)(2,1)S(1)} custom-call(s32[2]{0:T(128)S(1)} %pad_add_fusion.2.place, bf16[2,32,56,128]{3,2,1,0:T(8,128)(2,1)S(1)} %collective-permute-done.9.refs_0_, bf16[2,32,56,128]{3,2,1,0:T(8,128)(2,1)S(1)} %collective-permute-done.10.refs_1_), custom_call_target="tpu_custom_call" | custom-call | bytes 16777216 | tf_op jit(solution)/shard_map/pieces_diagonal/pallas_call | solution.py:269
  124.6 1.7 copy-done.3
  126.3 22.6 %experts.1 = (bf16[16,192,512]{2,1,0:T(8,128)(2,1)}, bf16[16,192,512]{2,1,0:T(8,128)(2,1)}) custom-call(s32[34]{0:T(128)} %pad_add_fusion.1.tab, f32[4,1024,128]{2,1,0:T(8,128)} %broadcast_in_dim.28.mix_ref, bf16[2048,384]{1,0:T(8,128)(2,1)} %copy-done.5, bf16[2048,384]{1,0:T(8,128)(2,1)} %copy-done.6, bf16[2048,384]{1,0:T(8,128)(2,1)} %copy-done.8, ...), custom_call_target="tpu_custom_call" | custom-call | tf_op jit(solution)/shard_map/experts/pallas_call | solution.py:297
  148.9 0.6 collective-permute-start.15
  149.5 5.5 %collective-permute-done.15 = bf16[16,192,512]{2,1,0:T(8,128)(2,1)S(1)} collective-permute-done((bf16[16,192,512]{2,1,0:T(8,128)(2,1)}, bf16[16,192,512]{2,1,0:T(8,128)(2,1)S(1)}, u32[]{:S(2)}, u32[]{:S(2)}) %collective-permute-start.15) | collective-permute-done | bytes 3145760 | tf_op jit(solution)/shard_map/ppermute | solution.py:317
  155.0 2.9 %add_convert_fusion = bf16[16,192,512]{2,1,0:T(8,128)(2,1)S(1)} fusion(bf16[16,192,512]{2,1,0:T(8,128)(2,1)S(1)} %collective-permute-done.15, bf16[16,192,512]{2,1,0:T(8,128)(2,1)} %get-tuple-element.55), kind=kLoop, calls=%fused_computation.1 | loop fusion | flops 6291456 | bytes 9437184 | tf_op jit(solution)/shard_map/convert_element_type | solution.py:318
  157.9 47.9 %all_to_all.10 = bf16[16,192,512]{2,1,0:T(8,128)(2,1)S(1)} all-to-all(bf16[16,192,512]{2,1,0:T(8,128)(2,1)S(1)} %add_convert_fusion), channel_id=1, replica_groups=mesh['zl'=2,'xh'=2,'xl'=2,'zh'=2,'y'=4,'core'=2] {'xh','zh','y'}, dimensions={0} | all-to-all | bytes 6291456 | tf_op jit(solution)/shard_map/all_to_all | solution.py:319
  206.2 0.7 reshape.148
  (51 shorter events, 4.0 us)
Async XLA Ops:
  1.7 24.5 %collective-permute-start.2 = (bf16[192,512]{1,0:T(8,128)(2,1)}, bf16[192,512]{1,0:T(8,128)(2,1)}, u32[]{:S(2)}, u32[]{:S(2)}) collective-permute-start(bf16[192,512]{1,0:T(8,128)(2,1)} %bitcast.8), channel_id=1, source_target_pairs={{0,40},{8,32},{32,8},{40,0},{1,41},{9,33},{33,9},{41,1},{2,42},{10... | collective-permute-start | bytes 589832 | tf_op jit(solution)/shard_map/ppermute | solution.py:207
  7.1 19.1 %collective-permute-start.1 = (bf16[192,512]{1,0:T(8,128)(2,1)}, bf16[192,512]{1,0:T(8,128)(2,1)}, u32[]{:S(2)}, u32[]{:S(2)}) collective-permute-start(bf16[192,512]{1,0:T(8,128)(2,1)} %bitcast.8), channel_id=1, source_target_pairs={{0,32},{32,0},{1,33},{33,1},{2,34},{34,2},{3,35},{35,3},{4,36},{36... | collective-permute-start | bytes 589832 | tf_op jit(solution)/shard_map/ppermute | solution.py:206
  7.6 18.6 %collective-permute-start = (bf16[192,512]{1,0:T(8,128)(2,1)}, bf16[192,512]{1,0:T(8,128)(2,1)}, u32[]{:S(2)}, u32[]{:S(2)}) collective-permute-start(bf16[192,512]{1,0:T(8,128)(2,1)} %bitcast.8), channel_id=1, source_target_pairs={{0,8},{8,0},{1,9},{9,1},{2,10},{10,2},{3,11},{11,3},{4,12},{12,4},... | collective-permute-start | bytes 589832 | tf_op jit(solution)/shard_map/ppermute | solution.py:206
  8.9 16.7 %collective-permute-start.3 = (f32[4,512]{1,0:T(4,128)S(1)}, f32[4,512]{1,0:T(4,128)S(1)}, u32[]{:S(2)}, u32[]{:S(2)}) collective-permute-start(f32[4,512]{1,0:T(4,128)S(1)} %select_reduce_fusion), channel_id=1, source_target_pairs={{0,32},{32,0},{1,33},{33,1},{2,34},{34,2},{3,35},{35,3},{4,36},{36... | collective-permute-start | bytes 24584 | tf_op jit(solution)/shard_map/ppermute | solution.py:219
  24.3 1.3 copy-start.4
  26.2 34.7 %all-to-all-start = ((bf16[32,4,56,128]{3,2,1,0:T(8,128)(2,1)}), bf16[32,4,56,128]{3,2,1,0:T(8,128)(2,1)S(1)}, u32[]{:S(2)}, u32[]{:S(2)}) async-start(bf16[32,4,56,128]{3,2,1,0:T(8,128)(2,1)} %copy-done.4), calls=%async_computation | async-start | bytes 3670016 | tf_op jit(solution)/shard_map/all_to_all | solution.py:249
  63.3 26.2 %collective-permute-start.7 = (bf16[2,32,56,128]{3,2,1,0:T(8,128)(2,1)}, bf16[2,32,56,128]{3,2,1,0:T(8,128)(2,1)S(1)}, u32[]{:S(2)}, u32[]{:S(2)}) collective-permute-start(bf16[2,32,56,128]{3,2,1,0:T(8,128)(2,1)} %bitcast.49), channel_id=1, source_target_pairs={{64,0},{8,64},{72,8},{0,72},{65,1},{9,65},{73,9},{1,73},{66,2},{10... | collective-permute-start | bytes 2752520 | tf_op jit(solution)/shard_map/ppermute | solution.py:262
  64.3 25.1 %collective-permute-start.8 = (bf16[2,32,56,128]{3,2,1,0:T(8,128)(2,1)}, bf16[2,32,56,128]{3,2,1,0:T(8,128)(2,1)}, u32[]{:S(2)}, u32[]{:S(2)}) collective-permute-start(bf16[2,32,56,128]{3,2,1,0:T(8,128)(2,1)} %bitcast.48), channel_id=1, source_target_pairs={{0,64},{64,8},{8,72},{72,0},{1,65},{65,9},{9,73},{73,1},{2,66},{66... | collective-permute-start | bytes 2752520 | tf_op jit(solution)/shard_map/ppermute | solution.py:262
  67.3 22.4 %collective-permute-start.5 = (bf16[2,32,56,128]{3,2,1,0:T(8,128)(2,1)}, bf16[2,32,56,128]{3,2,1,0:T(8,128)(2,1)}, u32[]{:S(2)}, u32[]{:S(2)}) collective-permute-start(bf16[2,32,56,128]{3,2,1,0:T(8,128)(2,1)} %bitcast.51), channel_id=1, source_target_pairs={{0,48},{16,0},{32,16},{48,32},{1,49},{17,1},{33,17},{49,33},{2,50}... | collective-permute-start | bytes 2752520 | tf_op jit(solution)/shard_map/ppermute | solution.py:259
  68.6 23.6 %collective-permute-start.6 = (bf16[2,32,56,128]{3,2,1,0:T(8,128)(2,1)}, bf16[2,32,56,128]{3,2,1,0:T(8,128)(2,1)}, u32[]{:S(2)}, u32[]{:S(2)}) collective-permute-start(bf16[2,32,56,128]{3,2,1,0:T(8,128)(2,1)} %bitcast.50), channel_id=1, source_target_pairs={{0,16},{16,32},{32,48},{48,0},{1,17},{17,33},{33,49},{49,1},{2,18}... | collective-permute-start | bytes 2752520 | tf_op jit(solution)/shard_map/ppermute | solution.py:259
  70.5 21.6 %copy-start.7 = (bf16[1024,384]{1,0:T(8,128)(2,1)S(1)}, bf16[1024,384]{1,0:T(8,128)(2,1)}, u32[]{:S(2)}) copy-start(bf16[1024,384]{1,0:T(8,128)(2,1)} %copy.57) | copy-start | bytes 2359300
  70.5 18.9 %collective-permute-start.4 = (bf16[1024,384]{1,0:T(8,128)(2,1)}, bf16[1024,384]{1,0:T(8,128)(2,1)S(1)}, u32[]{:S(2)}, u32[]{:S(2)}) collective-permute-start(bf16[1024,384]{1,0:T(8,128)(2,1)} %copy.57), channel_id=1, source_target_pairs={{0,6},{2,0},{4,2},{6,4},{1,7},{3,1},{5,3},{7,5},{8,14},{10,8},{12,... | collective-permute-start | bytes 2359304 | tf_op jit(solution)/shard_map/ppermute | solution.py:279
  77.6 16.5 %copy-start = (bf16[2,4,768,256]{3,2,1,0:T(8,128)(2,1)}, bf16[2,4,768,256]{3,2,1,0:T(8,128)(2,1)S(1)}, u32[]{:S(2)}) copy-start(bf16[2,4,768,256]{3,2,1,0:T(8,128)(2,1)S(1)} %pieces_here.1.refs_4_) | copy-start | bytes 9437188
  92.3 2.4 %copy-start.5 = (bf16[2048,384]{1,0:T(8,128)(2,1)}, bf16[2048,384]{1,0:T(8,128)(2,1)S(1)}, u32[]{:S(2)}) copy-start(bf16[2048,384]{1,0:T(8,128)(2,1)S(1)} %pad_maximum_fusion.refs_0_) | copy-start | bytes 4718596
  92.3 25.7 %collective-permute-start.13 = (bf16[2048,384]{1,0:T(8,128)(2,1)S(1)}, bf16[2048,384]{1,0:T(8,128)(2,1)S(1)}, u32[]{:S(2)}, u32[]{:S(2)}) collective-permute-start(bf16[2048,384]{1,0:T(8,128)(2,1)S(1)} %pad_maximum_fusion.refs_0_), channel_id=1, source_target_pairs={{0,1},{1,0},{2,3},{3,2},{4,5},{5,4},{6,7},{7,6},{8,9},{9,8},{10,11... | collective-permute-start | bytes 4718600 | tf_op jit(solution)/shard_map/ppermute | solution.py:288
  94.2 22.5 %collective-permute-start.9 = (bf16[2,32,56,128]{3,2,1,0:T(8,128)(2,1)S(1)}, bf16[2,32,56,128]{3,2,1,0:T(8,128)(2,1)S(1)}, u32[]{:S(2)}, u32[]{:S(2)}) collective-permute-start(bf16[2,32,56,128]{3,2,1,0:T(8,128)(2,1)S(1)} %pad_maximum_fusion.1), channel_id=1, source_target_pairs={{0,48},{16,0},{32,16},{48,32},{1,49},{17,1},{33,17},{49,33},{2,50}... | collective-permute-start | bytes 2752520 | tf_op jit(solution)/shard_map/ppermute | solution.py:259
  94.7 23.4 %collective-permute-start.10 = (bf16[2,32,56,128]{3,2,1,0:T(8,128)(2,1)S(1)}, bf16[2,32,56,128]{3,2,1,0:T(8,128)(2,1)S(1)}, u32[]{:S(2)}, u32[]{:S(2)}) collective-permute-start(bf16[2,32,56,128]{3,2,1,0:T(8,128)(2,1)S(1)} %pad_maximum_fusion.2), channel_id=1, source_target_pairs={{0,16},{16,32},{32,48},{48,0},{1,17},{17,33},{33,49},{49,1},{2,18}... | collective-permute-start | bytes 2752520 | tf_op jit(solution)/shard_map/ppermute | solution.py:259
  96.5 20.2 %collective-permute-start.11 = (bf16[1024,384]{1,0:T(8,128)(2,1)S(1)}, bf16[1024,384]{1,0:T(8,128)(2,1)S(1)}, u32[]{:S(2)}, u32[]{:S(2)}) collective-permute-start(bf16[1024,384]{1,0:T(8,128)(2,1)S(1)} %copy-done.7), channel_id=1, source_target_pairs={{0,2},{2,4},{4,6},{6,0},{1,3},{3,5},{5,7},{7,1},{8,10},{10,12},{12... | collective-permute-start | bytes 2359304 | tf_op jit(solution)/shard_map/ppermute | solution.py:286
  97.7 19.0 %collective-permute-start.12 = (bf16[1024,384]{1,0:T(8,128)(2,1)S(1)}, bf16[1024,384]{1,0:T(8,128)(2,1)S(1)}, u32[]{:S(2)}, u32[]{:S(2)}) collective-permute-start(bf16[1024,384]{1,0:T(8,128)(2,1)S(1)} %collective-permute-done.4), channel_id=1, source_target_pairs={{0,6},{2,0},{4,2},{6,4},{1,7},{3,1},{5,3},{7,5},{8,14},{10,8},{12,... | collective-permute-start | bytes 2359304 | tf_op jit(solution)/shard_map/ppermute | solution.py:286
  104.2 1.7 copy-start.1
  105.9 13.4 %copy-start.9 = (s32[16]{0:T(128)S(1)}, s32[16]{0:T(128)}, u32[]{:S(2)}) copy-start(s32[16]{0:T(128)} %param.12) | copy-start | bytes 196
  110.9 1.7 copy-start.2
  118.1 1.2 copy-start.8
  119.3 7.0 %copy-start.6 = (bf16[2048,384]{1,0:T(8,128)(2,1)}, bf16[2048,384]{1,0:T(8,128)(2,1)S(1)}, u32[]{:S(2)}) copy-start(bf16[2048,384]{1,0:T(8,128)(2,1)S(1)} %constant_dynamic-update-slice_fusion.refs_1_) | copy-start | bytes 4718596
  119.3 7.0 %collective-permute-start.14 = (bf16[2048,384]{1,0:T(8,128)(2,1)S(1)}, bf16[2048,384]{1,0:T(8,128)(2,1)}, u32[]{:S(2)}, u32[]{:S(2)}) collective-permute-start(bf16[2048,384]{1,0:T(8,128)(2,1)S(1)} %constant_dynamic-update-slice_fusion.refs_1_), channel_id=1, source_target_pairs={{0,1},{1,0},{2,3},{3,2},{4,5},{5,4},{6,7},{7,6},{8,9},{9,8},{10,11... | collective-permute-start | bytes 4718600 | tf_op jit(solution)/shard_map/ppermute | solution.py:292
  124.6 1.7 copy-start.3
  148.9 6.1 %collective-permute-start.15 = (bf16[16,192,512]{2,1,0:T(8,128)(2,1)}, bf16[16,192,512]{2,1,0:T(8,128)(2,1)S(1)}, u32[]{:S(2)}, u32[]{:S(2)}) collective-permute-start(bf16[16,192,512]{2,1,0:T(8,128)(2,1)} %get-tuple-element.56), channel_id=1, source_target_pairs={{0,1},{1,0},{2,3},{3,2},{4,5},{5,4},{6,7},{7,6},{8,9},{9,8},{10,11... | collective-permute-start | bytes 9437192 | tf_op jit(solution)/shard_map/ppermute | solution.py:317

commit v3 on v2

v3 whole, which is shorter than its diff:
```python
import functools

import jax
import jax.numpy as jnp
from jax import lax
from jax.experimental import pallas as pl
from jax.experimental.pallas import tpu as pltpu
from jax.sharding import Mesh
from jax.sharding import PartitionSpec as P

EXPERTS = 4
ROWS = 48
PART = 56
TOK = 512
HALF = 1536

learn_rate = 0.003
beta_one = 0.9
beta_two = 0.999
adam_eps = 1e-08
decay_rate = 0.1
bias_one = 1.0 - 0.9**20
bias_two = 1.0 - 0.999**20

bf16 = jnp.bfloat16
f32 = jnp.float32


def roll(x, by):
    if isinstance(by, int):
        by = by % 128
        if by == 0:
            return x
    return pltpu.roll(x, by, 1)


def pack_kernel(place, w_ref, o_ref):
    xl, zl = place[0], place[1]
    lane = lax.broadcasted_iota(jnp.int32, (ROWS, 128), 1)
    lane8 = lax.broadcasted_iota(jnp.int32, (8, 128), 1)
    within = lane % 64

    @pl.loop(0, 8)
    def _(k):
        def tile(s, kind, j):
            return w_ref[s, kind, :, pl.ds(pl.multiple_of(k * 384 + j * 128, 128), 128)].astype(f32)

        for i in range(16):
            a, off = (24 * i) // 128, (24 * i) % 128

            def source(s, kind):
                if off <= 104:
                    return tile(s, kind, a)
                return jnp.where(lane >= off, tile(s, kind, a), tile(s, kind, a + 1))

            pair = 2 * k + i // 8
            link_x, link_z = pair // 4, pair % 4
            jx, jz = (link_x + xl) % 2, (link_z + zl) % 2
            x_to, z_to = (link_x + jx) % 4, (link_z + jz) % 4
            to = (x_to // 2) * 16 + (z_to // 2) * 8 + i % 8
            halves, fold = [], jnp.zeros((8, 128), f32)
            for s in range(2):
                gate, up, down = source(s, 0), source(s, 1), source(s, 2)
                half = 64 * ((s + i // 8) % 2)
                gate, up = roll(gate, half - off), roll(up, half + 24 - off)
                main_down = roll(down, half + 48 - off)
                halves.append(jnp.where(within < 24, gate, jnp.where(within < 48, up, main_down)))
                for g in range(6):
                    at = 16 * g + 8 * s
                    rest = roll(down[8 * g : 8 * g + 8], at - off - 16)
                    fold = jnp.where((lane8 >= at) & (lane8 < at + 8), rest, fold)
            main = jnp.where(lane < 64, halves[i // 8], halves[1 - i // 8])
            o_ref[to, 2 * jx + jz] = jnp.concatenate([main, fold], 0).astype(bf16)


def assemble_kernel(along_x, place, *refs):
    *parts, o_ref = refs
    if len(parts) == 1:
        part = [lambda src, m=m: parts[0][src, m] for m in range(4)]
    elif along_x:
        part = [lambda src, m=m: parts[m // 2][m % 2, src] for m in range(4)]
    else:
        part = [lambda src, m=m: parts[m % 2][m // 2, src] for m in range(4)]
    lane = lax.broadcasted_iota(jnp.int32, (ROWS, 128), 1)
    lane8 = lax.broadcasted_iota(jnp.int32, (8, 128), 1)

    for zl in range(2):

        @pl.when(place[1] == zl)
        def _():
            @pl.loop(0, 32)
            def _(src):
                chunk = src % 16
                side = (chunk // 4 + place[2]) % 2
                row = (2 * side + chunk // 8) * 192 + (chunk % 4) * ROWS
                row = pl.ds(pl.multiple_of(row, ROWS), ROWS)
                loaded = [part[m](src).astype(f32) for m in range(4)]
                for slot in range(2):
                    swap = slot ^ zl
                    for pair in range(2):
                        first, second = loaded[2 * pair], loaded[2 * pair + 1]
                        main = roll(jnp.where((lane // 64) == swap, first[:ROWS], second[:ROWS]), swap * 64)
                        rows = []
                        for g in range(6):
                            at = 16 * g + 8 * slot
                            low, high = roll(second[ROWS:], -at), roll(first[ROWS:], 64 - at)
                            cur = main[8 * g : 8 * g + 8]
                            rows.append(jnp.where(lane8 < 8, low, jnp.where((lane8 // 8) == 8, high, cur)))
                        col = slice(pair * 128, pair * 128 + 128)
                        piece = (src // 16) * 2 + slot
                        o_ref[0, piece, row, col] = main.astype(bf16)
                        o_ref[1, piece, row, col] = jnp.concatenate(rows, 0).astype(bf16)


def fetch_pieces(tab, ws, use, experts, start):
    @pl.loop(4 * experts[0], 4 * experts[1])
    def _(i):
        src, slot = tab[2 * i], tab[2 * i + 1]
        for relation in range(4):

            @pl.when(src // 2 == relation)
            def _():
                start(i // 4, i % 4, ws[relation].at[use, (src % 2) * 2 + slot])


def wait_all(ref, sem):
    pltpu.make_async_copy(ref, ref, sem).wait()


def fetch_down(tab, ws, wd, dsem, side):
    def start(e, b, block):
        to = wd.at[pl.ds(2 * (b % 2), 2), b // 2, :, pl.ds(pl.multiple_of(e * 256, 256), 256)]
        pltpu.make_async_copy(block.at[side], to, dsem).start()

    fetch_pieces(tab, ws, 1, (0, EXPERTS), start)


def down(wd, hid, stage, osem, out_ref):
    for n in range(2):
        rows = wd[2 * n : 2 * n + 2].reshape(768, EXPERTS * 256)
        out = lax.dot_general(rows, hid[...], (((1,), (1,)), ((), ())), preferred_element_type=f32)
        stage[n] = out.astype(bf16)
        for q in range(4):
            for z in range(2):
                at = 8 * z + 4 * (q % 2) + 2 * n + q // 2
                block = stage.at[n, pl.ds(q * 192, 192), pl.ds(z * TOK, TOK)]
                pltpu.make_async_copy(block, out_ref.at[at], osem.at[n]).start()
    for n in range(2):
        wait_all(stage.at[n], osem.at[n])


def hidden_kernel(tab, *refs):
    xs, ws, mix_ref, (send_ref, hid, wd_own) = refs[:8], refs[8:12], refs[12], refs[13:16]
    x, wg, wd, stage, mix, xsem, gsem, dsem, osem, msem = refs[16:]
    y = tab[32]

    def start(e, b, block):
        to = wg.at[e, :, pl.ds(2 * (b % 2), 2), b // 2]
        pltpu.make_async_copy(block, to, gsem.at[e]).start()

    gets = []
    for side in range(2):
        for n, ref in enumerate(xs[4 * side : 4 * side + 4]):
            lanes = pl.ds(pl.multiple_of(side * HALF + ((y + n) % 4) * 384, 128), 384)
            gets.append(pltpu.make_async_copy(ref, x.at[:, lanes], xsem.at[len(gets)]))
            gets[-1].start()
    fetch_pieces(tab, ws, 0, (0, EXPERTS), start)
    gets.append(pltpu.make_async_copy(mix_ref, mix, msem))
    gets[-1].start()
    fetch_down(tab, ws, wd, dsem.at[1], 1)
    fetch_down(tab, ws, wd_own, dsem.at[0], 0)
    for get in gets:
        get.wait()

    lanes = lax.broadcasted_iota(jnp.int32, (2 * TOK, 128), 1) % 64

    @pl.loop(0, EXPERTS)
    def _(e):
        wait_all(wg.at[e], gsem.at[e])
        acc = jnp.dot(x[...], wg[e].reshape(2 * HALF, 256), preferred_element_type=f32)
        for n in range(2):
            gate = acc[:, n * 128 : (n + 1) * 128]
            hidden = (pltpu.roll(gate, 104, 1) + 1.0) * gate * jax.nn.sigmoid(1.702 * gate)
            hidden = hidden.astype(bf16).astype(f32) * mix[e]
            hidden = jnp.where((lanes >= 48) | (lanes < 8), pltpu.roll(hidden, 48, 1), 0.0)
            hid[:, pl.ds(pl.multiple_of(e * 256 + n * 128, 128), 128)] = hidden.astype(bf16)

    wait_all(wd, dsem.at[1])
    down(wd, hid, stage, osem, send_ref)
    wait_all(wd_own, dsem.at[0])


def own_kernel(wd, hid, own_ref, stage, osem):
    down(wd, hid, stage, osem, own_ref)


def update(master, moment_one, moment_two, gradient):
    moment_new = beta_one * moment_one + (1.0 - beta_one) * gradient
    second_new = beta_two * moment_two + (1.0 - beta_two) * gradient * gradient
    adjust = (
        moment_new / bias_one / (jnp.sqrt(second_new / bias_two) + adam_eps) + decay_rate * master
    )
    updated = (master - learn_rate * adjust).astype(bf16)
    return jnp.pad(updated.transpose(0, 2, 1, 3), ((0, 0), (0, 0), (0, ROWS - 45), (0, 3072 - 2880)))


def shards(master, moment_one, moment_two, gradient, piece_owner, tokens, routes, mix_weight):
    xl, zl, core = lax.axis_index("xl"), lax.axis_index("zl"), lax.axis_index("core")
    chips = ("xh", "zh", "y")
    swap = ((0, 1), (1, 0))
    plus = [(i, (i + 1) % 4) for i in range(4)]
    minus = [(i, (i - 1) % 4) for i in range(4)]

    own_x = tokens.transpose(2, 0, 1).reshape(4, 45, TOK)
    own_x = jnp.pad(own_x, ((0, 0), (0, ROWS - 45), (0, 0))).reshape(4 * ROWS, TOK)
    xh, zh = lax.axis_index("xh"), lax.axis_index("zh")
    at_z, at_x = lax.ppermute(own_x, "zh", swap), lax.ppermute(own_x, "xh", swap)
    def in_order(first, here, other):
        return jnp.stack([jnp.where(first, here, other), jnp.where(first, other, here)])


    flat_routes = routes.reshape(TOK, 2)
    flat_mix = mix_weight.reshape(TOK, 2)
    mine = jnp.sum(
        jnp.where(flat_routes[None] == jnp.arange(EXPERTS, dtype=jnp.int32)[:, None, None], flat_mix[None], 0.0), axis=2
    )
    updated = update(master, moment_one, moment_two, gradient)
    updated, at_x, mine = lax.optimization_barrier((updated, at_x, mine))
    swapped = own_x, at_z, at_x, lax.ppermute(at_x, "zh", swap)
    theirs = lax.ppermute(mine, "xh", swap)

    inverse = jnp.zeros((16,), jnp.int32).at[piece_owner].set(jnp.arange(16, dtype=jnp.int32))
    grp = inverse // 2
    relation = ((grp % 2) ^ xl) * 2 + ((grp // 4) ^ zl)
    source = relation * 2 + (grp % 4) // 2
    tab = jnp.concatenate([jnp.stack([source, inverse % 2], 1).reshape(-1), lax.axis_index("y").reshape(1)]).astype(jnp.int32)
    place = jnp.stack([xl, zl, core]).astype(jnp.int32)

    smem, vmem = pl.BlockSpec(memory_space=pltpu.SMEM), pl.BlockSpec(memory_space=pltpu.VMEM)
    packed = pl.pallas_call(
        pack_kernel,
        out_shape=jax.ShapeDtypeStruct((32, 4, PART, 128), bf16),
        in_specs=[smem, vmem],
        out_specs=vmem,
        compiler_params=pltpu.CompilerParams(vmem_limit_bytes=16 * 2**20),
        name="pack",
    )(place, updated)
    packed, swapped, theirs = lax.optimization_barrier((packed, swapped, theirs))
    w0 = lax.all_to_all(packed, ("xh", "zh", "y", "core"), 0, 0)
    held = in_order(xh == 0, in_order(zh == 0, *swapped[:2]), in_order(zh == 0, *swapped[2:]))
    held = held.transpose(0, 3, 1, 2).reshape(2 * TOK, 384)

    ax, az = ("xh", "xl"), ("zl", "zh")
    plus_z = [((i % 2) * 2 + i // 2, (j % 2) * 2 + j // 2) for i, j in plus]
    minus_z = [(j, i) for i, j in plus_z]

    def along_x(block, i):
        return lax.ppermute(block, ax, plus if i else minus)

    def along_z(block, j):
        return lax.ppermute(block, az, plus_z if j else minus_z)

    grid = w0.reshape(32, 2, 2, PART, 128)
    from_x = [along_x(jnp.swapaxes(grid[:, 1 - i], 0, 1), i) for i in range(2)]
    from_z = [along_z(jnp.swapaxes(grid[:, :, 1 - j], 0, 1), j) for j in range(2)]

    def assemble(parts, name):
        return pl.pallas_call(
            functools.partial(assemble_kernel, name != "pieces_z"),
            out_shape=jax.ShapeDtypeStruct((2, 4, 768, 256), bf16),
            in_specs=[smem] + [vmem] * len(parts),
            out_specs=vmem,
            compiler_params=pltpu.CompilerParams(vmem_limit_bytes=16 * 2**20),
            cost_estimate=pl.CostEstimate(flops=0, bytes_accessed=16 * 2**20, transcendentals=0),
            name=name,
        )(place, *parts).reshape(2, 4, 2, 2, 192, 256)

    x_held = lax.ppermute(held, "core", swap)
    held, x_held = lax.optimization_barrier((held, x_held))
    above = lax.ppermute(held, "y", minus)
    mix = jnp.where(
        xh == 0, jnp.concatenate([mine, theirs], 1), jnp.concatenate([theirs, mine], 1)
    )
    mix = jnp.broadcast_to(mix[:, :, None], (EXPERTS, 2 * TOK, 128))
    place, mix, tab = lax.optimization_barrier((place, mix, tab))
    here = assemble([w0], "pieces_here")
    above, from_x, from_z, here = lax.optimization_barrier((above, from_x, from_z, here))

    diagonal = [along_x(jnp.stack([from_z[0][1 - i], from_z[1][1 - i]]), i) for i in range(2)]
    below, far = lax.ppermute(held, "y", plus), lax.ppermute(above, "y", minus)
    x_above = lax.ppermute(above, "core", swap)
    ws = [here, assemble(from_z, "pieces_z"), assemble(from_x, "pieces_x")]
    diagonal, below, far, x_above, ws = lax.optimization_barrier((diagonal, below, far, x_above, ws))
    x_below, x_far = lax.ppermute(below, "core", swap), lax.ppermute(far, "core", swap)
    ws.append(assemble(diagonal, "pieces_diagonal"))
    xs = [held, above, far, below, x_held, x_above, x_far, x_below]

    hbm, anywhere = pl.BlockSpec(memory_space=pltpu.HBM), pl.BlockSpec(memory_space=pl.ANY)
    sums = jax.ShapeDtypeStruct((16, 192, TOK), bf16)
    hidden = jax.ShapeDtypeStruct((2 * TOK, EXPERTS * 256), bf16)
    down_half = jax.ShapeDtypeStruct((4, 2, 192, EXPERTS * 256), bf16)
    dma = pltpu.SemaphoreType.DMA
    stage = pltpu.VMEM((2, 768, 2 * TOK), bf16)
    send, hidden, down_own = pl.pallas_call(
        hidden_kernel,
        out_shape=[sums, hidden, down_half],
        in_specs=[smem] + [hbm] * 13,
        out_specs=[hbm, vmem, vmem],
        scratch_shapes=[
            pltpu.VMEM((2 * TOK, 2 * HALF), bf16),
            pltpu.VMEM((EXPERTS, 2, 4, 2, 192, 256), bf16),
            pltpu.VMEM(down_half.shape, bf16),
            stage,
            pltpu.VMEM((EXPERTS, 2 * TOK, 128), f32),
            dma((8,)),
            dma((EXPERTS,)),
            dma((2,)),
            dma((2,)),
            dma,
        ],
        compiler_params=pltpu.CompilerParams(vmem_limit_bytes=40 * 2**20),
        name="hidden",
    )(tab, *xs, *ws, mix)
    other = lax.ppermute(send, "core", swap)
    own_sum = pl.pallas_call(
        own_kernel,
        out_shape=sums,
        in_specs=[vmem] * 2,
        out_specs=anywhere,
        scratch_shapes=[stage, dma((2,))],
        compiler_params=pltpu.CompilerParams(vmem_limit_bytes=24 * 2**20),
        cost_estimate=pl.CostEstimate(flops=2 * HALF * 2 * TOK * 1024, bytes_accessed=8 * 2**20, transcendentals=0),
        name="own_side",
    )(down_own, hidden)
    both = (own_sum.astype(f32) + other.astype(f32)).astype(bf16)
    parts = lax.all_to_all(both, chips, 0, 0)
    total = jnp.sum(parts.astype(f32), axis=0).astype(bf16)
    total = total.reshape(4, ROWS, TOK)[:, :45].reshape(180, 4, 128)
    return total.transpose(1, 2, 0)


def solution(mesh):
    fine = Mesh(mesh.devices.reshape(2, 2, 2, 2, 4, 2), ("zl", "xh", "xl", "zh", "y", "core"))
    grp, tp = ("zl", "xh", "xl"), ("zh", "y", "core")
    state = P(grp, tp, None, None)
    return jax.shard_map(
        shards,
        mesh=fine,
        in_specs=(state, state, state, state, P(), P(None, grp, tp), P(None, grp, None), P(None, grp, None)),
        out_specs=P(None, grp, tp),
        check_vma=False,
    )
```

time: 207 us -> 200 us (0.966)
  waiting for transfers between devices: 50.5 us -> 42.9 us
  other arithmetic: 14.8 us -> 10.6 us
    ppermute x1, waiting for transfers between devices: 5.5 us -> 0.01 us  [shards(): other = lax.ppermute(send, 'core', swap)]
    ppermute x3 -> x5, starting transfers between devices: 5.53 us -> 1.41 us  [the longest x1 0.63 us: shards(): swapped = (own_x, at_z, at_x, lax.ppermute(at_x, 'zh', swap))]
    ppermute x4, waiting for transfers between devices: 4.11 us -> 0.71 us  [along_x(): return lax.ppermute(block, ax, plus if i else minus)]
    unnamed x26 -> x33, local copies, waits for them, and re-layouts: 11.6 us -> 14.8 us
    ppermute x1, starting transfers between devices: 3.1 us -> 0.51 us  [shards(): theirs = lax.ppermute(mine, 'xh', swap)]
    ppermute x1, starting transfers between devices: 0.51 us -> 3.02 us  [shards(): lax.ppermute(own_x, 'xh', swap)]
    ppermute x1, starting transfers between devices: 0.55 us -> 3.06 us  [shards(): lax.ppermute(own_x, 'zh', swap)]
    ppermute x1, waiting for transfers between devices: 0.01 us -> 2.35 us  [shards(): lax.ppermute(above, 'y', minus)]
  transfers between devices with their start and end apart: 17 -> 19, of which waited for: 7 -> 6; matrix products, arithmetic and copies ran while one was open for 10% -> 9% of each run, Pallas kernels for 10% -> 13%
where the time goes in v3:
time: 200 us; the launch traced here: 199 us
  blocking collectives  49.4 us (25%)
  Pallas kernels  45 us (22%)
  waiting for transfers between devices  42.9 us (21%)
  starting transfers between devices  27.2 us (14%)
  local copies, waits for them, and re-layouts  23.2 us (12%)
  other arithmetic  10.6 us (5%)
    all_to_all x1, blocking collectives, shards(): parts = lax.all_to_all(both, chips, 0, 0)  49.4 us
    all_to_all x1, waiting for transfers between devices, shards(): w0 = lax.all_to_all(packed, ('xh', 'zh', 'y', 'core'), 0, 0)  23.8 us
    pallas_call x1, Pallas kernels, shards(): pl.pallas_call(hidden_kernel, out_shape=[sums, hidden, down_half], in_spe...  18.9 us
    pallas_call x4, Pallas kernels, assemble(): pl.pallas_call(functools.partial(assemble_kernel, name != 'pieces_z'), ou...  17.6 us
    unnamed x33, local copies, waits for them, and re-layouts  14.8 us
    ppermute x1, waiting for transfers between devices, shards(): above = lax.ppermute(held, 'y', minus)  12.3 us
    all_to_all x1, starting transfers between devices, shards(): w0 = lax.all_to_all(packed, ('xh', 'zh', 'y', 'core'), 0, 0)  9.47 us
    transpose x1, other arithmetic, update(): updated.transpose(0, 2, 1, 3)  7.67 us
  transfers between devices with their start and end apart: 19, of which 6 were waited for; matrix products, arithmetic and copies ran while one was open for 9% of the time, Pallas kernels for 13%

profile of v3, /device:TPU:32, one launch (start us, length us, event | category | flops | bytes accessed | tf_op | source)
XLA Modules:
  0.0 198.7 jit_solution(13480452234500690429)
XLA Ops:
  0.0 1.0 reshape.185
  1.0 3.1 %collective-permute-start.1 = (bf16[192,512]{1,0:T(8,128)(2,1)S(1)}, bf16[192,512]{1,0:T(8,128)(2,1)S(1)}, u32[]{:S(2)}, u32[]{:S(2)}) collective-permute-start(bf16[192,512]{1,0:T(8,128)(2,1)S(1)} %bitcast.68), channel_id=1, source_target_pairs={{0,8},{8,0},{1,9},{9,1},{2,10},{10,2},{3,11},{11,3},{4,12},{12,4},... | collective-permute-start | bytes 589832 | tf_op jit(solution)/shard_map/ppermute | solution.py:217
  4.1 3.0 %collective-permute-start = (bf16[192,512]{1,0:T(8,128)(2,1)S(1)}, bf16[192,512]{1,0:T(8,128)(2,1)S(1)}, u32[]{:S(2)}, u32[]{:S(2)}) collective-permute-start(bf16[192,512]{1,0:T(8,128)(2,1)S(1)} %bitcast.69), channel_id=1, source_target_pairs={{0,32},{32,0},{1,33},{33,1},{2,34},{34,2},{3,35},{35,3},{4,36},{36... | collective-permute-start | bytes 589832 | tf_op jit(solution)/shard_map/ppermute | solution.py:217
  7.1 7.7 %fusion.8 = bf16[2,3,45,2880]{3,2,1,0:T(8,128)(2,1)S(1)} fusion(f32[2,45,3,2880]{3,0,2,1:T(2,128)} %param.10, f32[2,45,3,2880]{3,0,2,1:T(2,128)} %param.11, f32[2,45,3,2880]{3,0,2,1:T(2,128)} %param.9, f32[2,45,3,2880]{3,0,2,1:T(2,128)} %param.8), kind=kLoop, calls=%fused_computation.14 | loop fusion | flops 12441600 | bytes 13996800 | tf_op jit(solution)/shard_map/transpose | solution.py:204
  15.5 0.6 collective-permute-start.2
  16.2 0.5 collective-permute-start.3
  16.7 4.3 %pack.1 = bf16[32,4,56,128]{3,2,1,0:T(8,128)(2,1)S(1)} custom-call(s32[3]{0:T(128)S(1)} %pad_add_fusion.1.place, bf16[2,3,48,3072]{3,2,1,0:T(8,128)(2,1)S(1)} %pad.8.w_ref), custom_call_target="tpu_custom_call" | custom-call | tf_op jit(solution)/shard_map/pack/pallas_call | solution.py:240
  21.1 1.3 copy-done.4
  22.3 0.9 collective-permute-done.2
  23.2 9.5 %all-to-all-start = ((bf16[32,4,56,128]{3,2,1,0:T(8,128)(2,1)}), bf16[32,4,56,128]{3,2,1,0:T(8,128)(2,1)S(1)}, u32[]{:S(2)}, u32[]{:S(2)}) async-start(bf16[32,4,56,128]{3,2,1,0:T(8,128)(2,1)} %copy-done.4), calls=%async_computation | async-start | bytes 3670016 | tf_op jit(solution)/shard_map/all_to_all | solution.py:249
  32.9 0.8 copy.52
  33.9 0.9 copy-done.8
  34.8 1.2 copy.53
  36.2 23.8 %all-to-all-done.refs_0_ = bf16[32,4,56,128]{3,2,1,0:T(8,128)(2,1)S(1)} async-done(((bf16[32,4,56,128]{3,2,1,0:T(8,128)(2,1)}), bf16[32,4,56,128]{3,2,1,0:T(8,128)(2,1)S(1)}, u32[]{:S(2)}, u32[]{:S(2)}) %all-to-all-start) | async-done | bytes 1835040 | tf_op jit(solution)/shard_map/all_to_all | solution.py:249
  60.2 1.0 copy.94
  61.2 1.1 copy.95
  62.3 1.0 collective-permute-start.8
  63.3 1.0 collective-permute-start.9
  64.5 1.0 copy.96
  65.5 1.0 copy.97
  66.9 1.6 collective-permute-start.7
  68.5 0.9 copy-done.5
  69.5 1.5 copy.60.refs_0_
  71.1 0.6 scatter_custom_fusion
  72.0 0.8 maximum_select_fusion
  72.8 0.6 broadcast_in_dim.27.refs_12_
  73.4 4.0 %pieces_here.1 = bf16[2,4,768,256]{3,2,1,0:T(8,128)(2,1)S(1)} custom-call(s32[3]{0:T(128)S(1)} %pad_add_fusion.1.place, bf16[32,4,56,128]{3,2,1,0:T(8,128)(2,1)S(1)} %all-to-all-done.refs_0_), custom_call_target="tpu_custom_call" | custom-call | bytes 16777216 | tf_op jit(solution)/shard_map/pieces_here/pallas_call | solution.py:268
  77.5 12.3 %collective-permute-done.5.refs_1_ = bf16[1024,384]{1,0:T(8,128)(2,1)} collective-permute-done((bf16[1024,384]{1,0:T(8,128)(2,1)S(1)}, bf16[1024,384]{1,0:T(8,128)(2,1)}, u32[]{:S(2)}, u32[]{:S(2)}) %collective-permute-start.5) | collective-permute-done | bytes 786464 | tf_op jit(solution)/shard_map/ppermute | solution.py:280
  89.8 0.7 collective-permute-done.7.refs_1_
  90.6 1.2 fusion.15
  91.9 1.3 collective-permute-start.10
  93.3 0.9 collective-permute-start.11
  94.2 1.2 collective-permute-start.12
  95.4 2.0 %collective-permute-start.13 = (bf16[1024,384]{1,0:T(8,128)(2,1)}, bf16[1024,384]{1,0:T(8,128)(2,1)S(1)}, u32[]{:S(2)}, u32[]{:S(2)}) collective-permute-start(bf16[1024,384]{1,0:T(8,128)(2,1)} %collective-permute-done.5.refs_1_), channel_id=1, source_target_pairs={{0,6},{2,0},{4,2},{6,4},{1,7},{3,1},{5,3},{7,5},{8,14},{10,8},{12,... | collective-permute-start | bytes 2359304 | tf_op jit(solution)/shard_map/ppermute | solution.py:290
  97.4 4.7 %pieces_z.1 = bf16[2,4,768,256]{3,2,1,0:T(8,128)(2,1)S(1)} custom-call(s32[3]{0:T(128)S(1)} %pad_add_fusion.1.place, bf16[2,32,56,128]{3,2,1,0:T(8,128)(2,1)S(1)} %collective-permute-done.8.refs_0_, bf16[2,32,56,128]{3,2,1,0:T(8,128)(2,1)} %collective-permute-done.9.refs_1_), custom_call_target="tpu_custom_call" | custom-call | bytes 16777216 | tf_op jit(solution)/shard_map/pieces_z/pallas_call | solution.py:268
  102.1 1.7 copy-done.1
  103.8 4.9 %pieces_x.1 = bf16[2,4,768,256]{3,2,1,0:T(8,128)(2,1)S(1)} custom-call(s32[3]{0:T(128)S(1)} %pad_add_fusion.1.place, bf16[2,32,56,128]{3,2,1,0:T(8,128)(2,1)} %collective-permute-done.6.refs_0_, bf16[2,32,56,128]{3,2,1,0:T(8,128)(2,1)} %collective-permute-done.7.refs_1_), custom_call_target="tpu_custom_call" | custom-call | bytes 16777216 | tf_op jit(solution)/shard_map/pieces_x/pallas_call | solution.py:268
  108.7 1.7 copy-done.2
  110.5 2.7 %collective-permute-done.12.refs_3_ = bf16[1024,384]{1,0:T(8,128)(2,1)S(1)} collective-permute-done((bf16[1024,384]{1,0:T(8,128)(2,1)S(1)}, bf16[1024,384]{1,0:T(8,128)(2,1)S(1)}, u32[]{:S(2)}, u32[]{:S(2)}) %collective-permute-start.12) | collective-permute-done | bytes 786464 | tf_op jit(solution)/shard_map/ppermute | solution.py:290
  113.2 2.4 %collective-permute-done.13.refs_2_ = bf16[1024,384]{1,0:T(8,128)(2,1)S(1)} collective-permute-done((bf16[1024,384]{1,0:T(8,128)(2,1)}, bf16[1024,384]{1,0:T(8,128)(2,1)S(1)}, u32[]{:S(2)}, u32[]{:S(2)}) %collective-permute-start.13) | collective-permute-done | bytes 786464 | tf_op jit(solution)/shard_map/ppermute | solution.py:290
  116.1 4.0 %pieces_diagonal.1 = bf16[2,4,768,256]{3,2,1,0:T(8,128)(2,1)S(1)} custom-call(s32[3]{0:T(128)S(1)} %pad_add_fusion.1.place, bf16[2,32,56,128]{3,2,1,0:T(8,128)(2,1)S(1)} %collective-permute-done.10.refs_0_, bf16[2,32,56,128]{3,2,1,0:T(8,128)(2,1)S(1)} %collective-permute-done.11.refs_1_), custom_call_target="tpu_custom_call" | custom-call | bytes 16777216 | tf_op jit(solution)/shard_map/pieces_diagonal/pallas_call | solution.py:268
  120.1 1.7 copy-done.3
  121.8 18.9 %hidden.1 = (bf16[16,192,512]{2,1,0:T(8,128)(2,1)S(1)}, bf16[1024,1024]{1,0:T(8,128)(2,1)S(1)}, bf16[4,2,192,1024]{3,2,1,0:T(8,128)(2,1)}) custom-call(s32[33]{0:T(128)S(1)} %pad_add_fusion.2.tab, bf16[1024,384]{1,0:T(8,128)(2,1)S(1)} %copy.60.refs_0_, bf16[1024,384]{1,0:T(8,128)(2,1)} %collective-permute-done.5.refs_1_, ...), custom_call_target="tpu_custom_call" | custom-call | tf_op jit(solution)/shard_map/hidden/pallas_call | solution.py:304
  140.9 1.9 copy-done.7
  142.8 4.2 %own_side.1 = bf16[16,192,512]{2,1,0:T(8,128)(2,1)S(1)} custom-call(bf16[4,2,192,1024]{3,2,1,0:T(8,128)(2,1)S(1)} %copy-done.7, bf16[1024,1024]{1,0:T(8,128)(2,1)S(1)} %get-tuple-element.65.hid), custom_call_target="tpu_custom_call" | custom-call | flops 3221225472 | bytes 8388608 | tf_op jit(solution)/shard_map/own_side/pallas_call | solution.py:325
  146.9 1.1 add_convert_fusion
  148.1 49.4 %all_to_all.10 = bf16[16,192,512]{2,1,0:T(8,128)(2,1)S(1)} all-to-all(bf16[16,192,512]{2,1,0:T(8,128)(2,1)S(1)} %add_convert_fusion), channel_id=1, replica_groups=mesh['zl'=2,'xh'=2,'xl'=2,'zh'=2,'y'=4,'core'=2] {'xh','zh','y'}, dimensions={0} | all-to-all | bytes 6291456 | tf_op jit(solution)/shard_map/all_to_all | solution.py:336
  197.9 0.7 reshape.196
  (62 shorter events, 3.9 us)
Async XLA Ops:
  1.0 21.3 %collective-permute-start.1 = (bf16[192,512]{1,0:T(8,128)(2,1)S(1)}, bf16[192,512]{1,0:T(8,128)(2,1)S(1)}, u32[]{:S(2)}, u32[]{:S(2)}) collective-permute-start(bf16[192,512]{1,0:T(8,128)(2,1)S(1)} %bitcast.68), channel_id=1, source_target_pairs={{0,8},{8,0},{1,9},{9,1},{2,10},{10,2},{3,11},{11,3},{4,12},{12,4},... | collective-permute-start | bytes 589832 | tf_op jit(solution)/shard_map/ppermute | solution.py:217
  4.1 11.4 %collective-permute-start = (bf16[192,512]{1,0:T(8,128)(2,1)S(1)}, bf16[192,512]{1,0:T(8,128)(2,1)S(1)}, u32[]{:S(2)}, u32[]{:S(2)}) collective-permute-start(bf16[192,512]{1,0:T(8,128)(2,1)S(1)} %bitcast.69), channel_id=1, source_target_pairs={{0,32},{32,0},{1,33},{33,1},{2,34},{34,2},{3,35},{35,3},{4,36},{36... | collective-permute-start | bytes 589832 | tf_op jit(solution)/shard_map/ppermute | solution.py:217
  14.8 0.7 copy-start.11
  14.8 0.7 copy-start.12
  15.5 7.7 %copy-start.9 = (f32[4,512]{1,0:T(4,128)}, f32[4,512]{1,0:T(4,128)S(1)}, u32[]{:S(2)}) copy-start(f32[4,512]{1,0:T(4,128)S(1)} %select_reduce_fusion) | copy-start | bytes 24580
  15.5 7.7 %collective-permute-start.2 = (bf16[192,512]{1,0:T(8,128)(2,1)S(1)}, bf16[192,512]{1,0:T(8,128)(2,1)S(1)}, u32[]{:S(2)}, u32[]{:S(2)}) collective-permute-start(bf16[192,512]{1,0:T(8,128)(2,1)S(1)} %collective-permute-done), channel_id=1, source_target_pairs={{0,8},{8,0},{1,9},{9,1},{2,10},{10,2},{3,11},{11,3},{4,12},{12,4},... | collective-permute-start | bytes 589832 | tf_op jit(solution)/shard_map/ppermute | solution.py:229
  16.2 6.2 %collective-permute-start.3 = (f32[4,512]{1,0:T(4,128)S(1)}, f32[4,512]{1,0:T(4,128)S(1)}, u32[]{:S(2)}, u32[]{:S(2)}) collective-permute-start(f32[4,512]{1,0:T(4,128)S(1)} %select_reduce_fusion), channel_id=1, source_target_pairs={{0,32},{32,0},{1,33},{33,1},{2,34},{34,2},{3,35},{35,3},{4,36},{36... | collective-permute-start | bytes 24584 | tf_op jit(solution)/shard_map/ppermute | solution.py:230
  21.1 1.3 copy-start.4
  22.3 0.9 copy-start.10
  23.2 36.8 %all-to-all-start = ((bf16[32,4,56,128]{3,2,1,0:T(8,128)(2,1)}), bf16[32,4,56,128]{3,2,1,0:T(8,128)(2,1)S(1)}, u32[]{:S(2)}, u32[]{:S(2)}) async-start(bf16[32,4,56,128]{3,2,1,0:T(8,128)(2,1)} %copy-done.4), calls=%async_computation | async-start | bytes 3670016 | tf_op jit(solution)/shard_map/all_to_all | solution.py:249
  33.9 0.9 copy-start.8
  35.9 32.6 %collective-permute-start.4 = (bf16[1024,384]{1,0:T(8,128)(2,1)}, bf16[1024,384]{1,0:T(8,128)(2,1)S(1)}, u32[]{:S(2)}, u32[]{:S(2)}) collective-permute-start(bf16[1024,384]{1,0:T(8,128)(2,1)} %copy.53), channel_id=1, source_target_pairs={{0,1},{1,0},{2,3},{3,2},{4,5},{5,4},{6,7},{7,6},{8,9},{9,8},{10,11... | collective-permute-start | bytes 2359304 | tf_op jit(solution)/shard_map/ppermute | solution.py:278
  62.3 27.5 %collective-permute-start.8 = (bf16[2,32,56,128]{3,2,1,0:T(8,128)(2,1)}, bf16[2,32,56,128]{3,2,1,0:T(8,128)(2,1)S(1)}, u32[]{:S(2)}, u32[]{:S(2)}) collective-permute-start(bf16[2,32,56,128]{3,2,1,0:T(8,128)(2,1)} %bitcast.53), channel_id=1, source_target_pairs={{64,0},{8,64},{72,8},{0,72},{65,1},{9,65},{73,9},{1,73},{66,2},{10... | collective-permute-start | bytes 2752520 | tf_op jit(solution)/shard_map/ppermute | solution.py:261
  63.3 26.5 %collective-permute-start.9 = (bf16[2,32,56,128]{3,2,1,0:T(8,128)(2,1)}, bf16[2,32,56,128]{3,2,1,0:T(8,128)(2,1)}, u32[]{:S(2)}, u32[]{:S(2)}) collective-permute-start(bf16[2,32,56,128]{3,2,1,0:T(8,128)(2,1)} %bitcast.52), channel_id=1, source_target_pairs={{0,64},{64,8},{8,72},{72,0},{1,65},{65,9},{9,73},{73,1},{2,66},{66... | collective-permute-start | bytes 2752520 | tf_op jit(solution)/shard_map/ppermute | solution.py:261
  64.5 6.6 %copy-start.13 = (s32[16]{0:T(128)S(1)}, s32[16]{0:T(128)}, u32[]{:S(2)}) copy-start(s32[16]{0:T(128)} %param.12) | copy-start | bytes 196
  66.5 23.3 %collective-permute-start.6 = (bf16[2,32,56,128]{3,2,1,0:T(8,128)(2,1)}, bf16[2,32,56,128]{3,2,1,0:T(8,128)(2,1)}, u32[]{:S(2)}, u32[]{:S(2)}) collective-permute-start(bf16[2,32,56,128]{3,2,1,0:T(8,128)(2,1)} %bitcast.55), channel_id=1, source_target_pairs={{0,48},{16,0},{32,16},{48,32},{1,49},{17,1},{33,17},{49,33},{2,50}... | collective-permute-start | bytes 2752520 | tf_op jit(solution)/shard_map/ppermute | solution.py:258
  66.9 23.6 %collective-permute-start.7 = (bf16[2,32,56,128]{3,2,1,0:T(8,128)(2,1)}, bf16[2,32,56,128]{3,2,1,0:T(8,128)(2,1)}, u32[]{:S(2)}, u32[]{:S(2)}) collective-permute-start(bf16[2,32,56,128]{3,2,1,0:T(8,128)(2,1)} %bitcast.54), channel_id=1, source_target_pairs={{0,16},{16,32},{32,48},{48,0},{1,17},{17,33},{33,49},{49,1},{2,18}... | collective-permute-start | bytes 2752520 | tf_op jit(solution)/shard_map/ppermute | solution.py:258
  68.5 0.9 copy-start.5
  71.0 18.8 %collective-permute-start.5 = (bf16[1024,384]{1,0:T(8,128)(2,1)S(1)}, bf16[1024,384]{1,0:T(8,128)(2,1)}, u32[]{:S(2)}, u32[]{:S(2)}) collective-permute-start(bf16[1024,384]{1,0:T(8,128)(2,1)S(1)} %copy.60.refs_0_), channel_id=1, source_target_pairs={{0,6},{2,0},{4,2},{6,4},{1,7},{3,1},{5,3},{7,5},{8,14},{10,8},{12,... | collective-permute-start | bytes 2359304 | tf_op jit(solution)/shard_map/ppermute | solution.py:280
  77.4 15.9 %copy-start = (bf16[2,4,768,256]{3,2,1,0:T(8,128)(2,1)}, bf16[2,4,768,256]{3,2,1,0:T(8,128)(2,1)S(1)}, u32[]{:S(2)}) copy-start(bf16[2,4,768,256]{3,2,1,0:T(8,128)(2,1)S(1)} %pieces_here.1) | copy-start | bytes 9437188
  91.9 23.6 %collective-permute-start.10 = (bf16[2,32,56,128]{3,2,1,0:T(8,128)(2,1)S(1)}, bf16[2,32,56,128]{3,2,1,0:T(8,128)(2,1)S(1)}, u32[]{:S(2)}, u32[]{:S(2)}) collective-permute-start(bf16[2,32,56,128]{3,2,1,0:T(8,128)(2,1)S(1)} %pad_maximum_fusion), channel_id=1, source_target_pairs={{0,48},{16,0},{32,16},{48,32},{1,49},{17,1},{33,17},{49,33},{2,50}... | collective-permute-start | bytes 2752520 | tf_op jit(solution)/shard_map/ppermute | solution.py:258
  93.3 22.2 %collective-permute-start.11 = (bf16[2,32,56,128]{3,2,1,0:T(8,128)(2,1)S(1)}, bf16[2,32,56,128]{3,2,1,0:T(8,128)(2,1)S(1)}, u32[]{:S(2)}, u32[]{:S(2)}) collective-permute-start(bf16[2,32,56,128]{3,2,1,0:T(8,128)(2,1)S(1)} %pad_maximum_fusion.1), channel_id=1, source_target_pairs={{0,16},{16,32},{32,48},{48,0},{1,17},{17,33},{33,49},{49,1},{2,18}... | collective-permute-start | bytes 2752520 | tf_op jit(solution)/shard_map/ppermute | solution.py:258
  94.2 19.0 %collective-permute-start.12 = (bf16[1024,384]{1,0:T(8,128)(2,1)S(1)}, bf16[1024,384]{1,0:T(8,128)(2,1)S(1)}, u32[]{:S(2)}, u32[]{:S(2)}) collective-permute-start(bf16[1024,384]{1,0:T(8,128)(2,1)S(1)} %copy.60.refs_0_), channel_id=1, source_target_pairs={{0,2},{2,4},{4,6},{6,0},{1,3},{3,5},{5,7},{7,1},{8,10},{10,12},{12... | collective-permute-start | bytes 2359304 | tf_op jit(solution)/shard_map/ppermute | solution.py:290
  95.4 17.8 %collective-permute-start.14 = (bf16[1024,384]{1,0:T(8,128)(2,1)}, bf16[1024,384]{1,0:T(8,128)(2,1)S(1)}, u32[]{:S(2)}, u32[]{:S(2)}) collective-permute-start(bf16[1024,384]{1,0:T(8,128)(2,1)} %collective-permute-done.5.refs_1_), channel_id=1, source_target_pairs={{0,1},{1,0},{2,3},{3,2},{4,5},{5,4},{6,7},{7,6},{8,9},{9,8},{10,11... | collective-permute-start | bytes 2359304 | tf_op jit(solution)/shard_map/ppermute | solution.py:291
  95.4 20.2 %collective-permute-start.13 = (bf16[1024,384]{1,0:T(8,128)(2,1)}, bf16[1024,384]{1,0:T(8,128)(2,1)S(1)}, u32[]{:S(2)}, u32[]{:S(2)}) collective-permute-start(bf16[1024,384]{1,0:T(8,128)(2,1)} %collective-permute-done.5.refs_1_), channel_id=1, source_target_pairs={{0,6},{2,0},{4,2},{6,4},{1,7},{3,1},{5,3},{7,5},{8,14},{10,8},{12,... | collective-permute-start | bytes 2359304 | tf_op jit(solution)/shard_map/ppermute | solution.py:290
  102.1 1.7 copy-start.1
  108.7 1.7 copy-start.2
  110.5 11.3 %copy-start.6 = (bf16[1024,384]{1,0:T(8,128)(2,1)S(1)}, bf16[1024,384]{1,0:T(8,128)(2,1)}, u32[]{:S(2)}) copy-start(bf16[1024,384]{1,0:T(8,128)(2,1)} %copy-done.5) | copy-start | bytes 2359300
  115.6 6.2 %collective-permute-start.15 = (bf16[1024,384]{1,0:T(8,128)(2,1)S(1)}, bf16[1024,384]{1,0:T(8,128)(2,1)S(1)}, u32[]{:S(2)}, u32[]{:S(2)}) collective-permute-start(bf16[1024,384]{1,0:T(8,128)(2,1)S(1)} %collective-permute-done.13.refs_2_), channel_id=1, source_target_pairs={{0,1},{1,0},{2,3},{3,2},{4,5},{5,4},{6,7},{7,6},{8,9},{9,8},{10,11... | collective-permute-start | bytes 2359304 | tf_op jit(solution)/shard_map/ppermute | solution.py:294
  115.6 6.2 %collective-permute-start.16 = (bf16[1024,384]{1,0:T(8,128)(2,1)S(1)}, bf16[1024,384]{1,0:T(8,128)(2,1)S(1)}, u32[]{:S(2)}, u32[]{:S(2)}) collective-permute-start(bf16[1024,384]{1,0:T(8,128)(2,1)S(1)} %collective-permute-done.12.refs_3_), channel_id=1, source_target_pairs={{0,1},{1,0},{2,3},{3,2},{4,5},{5,4},{6,7},{7,6},{8,9},{9,8},{10,11... | collective-permute-start | bytes 2359304 | tf_op jit(solution)/shard_map/ppermute | solution.py:294
  120.1 1.7 copy-start.3
  140.7 6.2 %collective-permute-start.17 = (bf16[16,192,512]{2,1,0:T(8,128)(2,1)S(1)}, bf16[16,192,512]{2,1,0:T(8,128)(2,1)S(1)}, u32[]{:S(2)}, u32[]{:S(2)}) collective-permute-start(bf16[16,192,512]{2,1,0:T(8,128)(2,1)S(1)} %get-tuple-element.66), channel_id=1, source_target_pairs={{0,1},{1,0},{2,3},{3,2},{4,5},{5,4},{6,7},{7,6},{8,9},{9,8},{10,11... | collective-permute-start | bytes 9437192 | tf_op jit(solution)/shard_map/ppermute | solution.py:324
  140.9 1.9 copy-start.7

commit v4 on v3

--- a/solution.py
+++ b/solution.py
@@ -288,10 +288,11 @@
 
     diagonal = [along_x(jnp.stack([from_z[0][1 - i], from_z[1][1 - i]]), i) for i in range(2)]
     below, far = lax.ppermute(held, "y", plus), lax.ppermute(above, "y", minus)
-    x_above = lax.ppermute(above, "core", swap)
     ws = [here, assemble(from_z, "pieces_z"), assemble(from_x, "pieces_x")]
-    diagonal, below, far, x_above, ws = lax.optimization_barrier((diagonal, below, far, x_above, ws))
-    x_below, x_far = lax.ppermute(below, "core", swap), lax.ppermute(far, "core", swap)
+    below, above, ws = lax.optimization_barrier((below, above, ws))
+    x_below, x_above = lax.ppermute(below, "core", swap), lax.ppermute(above, "core", swap)
+    diagonal, far = lax.optimization_barrier((diagonal, far))
+    x_far = lax.ppermute(far, "core", swap)
     ws.append(assemble(diagonal, "pieces_diagonal"))
     xs = [held, above, far, below, x_held, x_above, x_far, x_below]
 
@@ -318,7 +319,7 @@
             dma((2,)),
             dma,
         ],
-        compiler_params=pltpu.CompilerParams(vmem_limit_bytes=40 * 2**20),
+        compiler_params=pltpu.CompilerParams(vmem_limit_bytes=34 * 2**20),
         name="hidden",
     )(tab, *xs, *ws, mix)
     other = lax.ppermute(send, "core", swap)

time: 200 us -> 195 us (0.975)
  local copies, waits for them, and re-layouts: 23.2 us -> 21.2 us
  blocking collectives: 49.4 us -> 47.4 us
    ppermute x1, waiting for transfers between devices: 2.35 us -> 0.01 us  [shards(): lax.ppermute(above, 'y', minus)]
    unnamed x33 -> x29, local copies, waits for them, and re-layouts: 14.8 us -> 12.7 us
  transfers between devices with their start and end apart: 19 -> 19, of which waited for: 6 -> 7; matrix products, arithmetic and copies ran while one was open for 9% -> 10% of each run, Pallas kernels for 13% -> 13%
where the time goes in v4:
time: 195 us; the launch traced here: 194 us
  blocking collectives  47.4 us (24%)
  Pallas kernels  43.8 us (22%)
  waiting for transfers between devices  43.2 us (22%)
  starting transfers between devices  27.6 us (14%)
  local copies, waits for them, and re-layouts  21.2 us (11%)
  other arithmetic  10.6 us (5%)
    all_to_all x1, blocking collectives, shards(): parts = lax.all_to_all(both, chips, 0, 0)  47.4 us
    all_to_all x1, waiting for transfers between devices, shards(): w0 = lax.all_to_all(packed, ('xh', 'zh', 'y', 'core'), 0, 0)  23.8 us
    pallas_call x1, Pallas kernels, shards(): pl.pallas_call(hidden_kernel, out_shape=[sums, hidden, down_half], in_spe...  17.7 us
    pallas_call x4, Pallas kernels, assemble(): pl.pallas_call(functools.partial(assemble_kernel, name != 'pieces_z'), ou...  17.6 us
    unnamed x29, local copies, waits for them, and re-layouts  12.7 us
    ppermute x1, waiting for transfers between devices, shards(): above = lax.ppermute(held, 'y', minus)  12.4 us
    all_to_all x1, starting transfers between devices, shards(): w0 = lax.all_to_all(packed, ('xh', 'zh', 'y', 'core'), 0, 0)  9.46 us
    transpose x1, other arithmetic, update(): updated.transpose(0, 2, 1, 3)  7.67 us
  transfers between devices with their start and end apart: 19, of which 7 were waited for; matrix products, arithmetic and copies ran while one was open for 10% of the time, Pallas kernels for 13%

profile of v4, /device:TPU:32, one launch (start us, length us, event | category | flops | bytes accessed | tf_op | source)
XLA Modules:
  0.0 194.2 jit_solution(10145230203248149628)
XLA Ops:
  0.0 1.0 reshape.185
  1.0 3.1 %collective-permute-start.1 = (bf16[192,512]{1,0:T(8,128)(2,1)S(1)}, bf16[192,512]{1,0:T(8,128)(2,1)S(1)}, u32[]{:S(2)}, u32[]{:S(2)}) collective-permute-start(bf16[192,512]{1,0:T(8,128)(2,1)S(1)} %bitcast.68), channel_id=1, source_target_pairs={{0,8},{8,0},{1,9},{9,1},{2,10},{10,2},{3,11},{11,3},{4,12},{12,4},... | collective-permute-start | bytes 589832 | tf_op jit(solution)/shard_map/ppermute | solution.py:217
  4.1 3.0 %collective-permute-start = (bf16[192,512]{1,0:T(8,128)(2,1)S(1)}, bf16[192,512]{1,0:T(8,128)(2,1)S(1)}, u32[]{:S(2)}, u32[]{:S(2)}) collective-permute-start(bf16[192,512]{1,0:T(8,128)(2,1)S(1)} %bitcast.69), channel_id=1, source_target_pairs={{0,32},{32,0},{1,33},{33,1},{2,34},{34,2},{3,35},{35,3},{4,36},{36... | collective-permute-start | bytes 589832 | tf_op jit(solution)/shard_map/ppermute | solution.py:217
  7.1 7.7 %fusion.8 = bf16[2,3,45,2880]{3,2,1,0:T(8,128)(2,1)S(1)} fusion(f32[2,45,3,2880]{3,0,2,1:T(2,128)} %param.10, f32[2,45,3,2880]{3,0,2,1:T(2,128)} %param.11, f32[2,45,3,2880]{3,0,2,1:T(2,128)} %param.9, f32[2,45,3,2880]{3,0,2,1:T(2,128)} %param.8), kind=kLoop, calls=%fused_computation.14 | loop fusion | flops 12441600 | bytes 13996800 | tf_op jit(solution)/shard_map/transpose | solution.py:204
  15.5 0.6 collective-permute-start.2
  16.7 4.3 %pack.1 = bf16[32,4,56,128]{3,2,1,0:T(8,128)(2,1)S(1)} custom-call(s32[3]{0:T(128)S(1)} %pad_add_fusion.1.place, bf16[2,3,48,3072]{3,2,1,0:T(8,128)(2,1)S(1)} %pad.8.w_ref), custom_call_target="tpu_custom_call" | custom-call | tf_op jit(solution)/shard_map/pack/pallas_call | solution.py:240
  21.1 1.2 copy-done.3
  22.3 0.9 collective-permute-done.2
  23.2 9.5 %all-to-all-start = ((bf16[32,4,56,128]{3,2,1,0:T(8,128)(2,1)}), bf16[32,4,56,128]{3,2,1,0:T(8,128)(2,1)S(1)}, u32[]{:S(2)}, u32[]{:S(2)}) async-start(bf16[32,4,56,128]{3,2,1,0:T(8,128)(2,1)} %copy-done.3), calls=%async_computation | async-start | bytes 3670016 | tf_op jit(solution)/shard_map/all_to_all | solution.py:249
  32.9 0.8 copy.52
  33.9 0.9 copy-done.6
  34.7 1.2 copy.53
  36.2 23.8 %all-to-all-done.refs_0_ = bf16[32,4,56,128]{3,2,1,0:T(8,128)(2,1)S(1)} async-done(((bf16[32,4,56,128]{3,2,1,0:T(8,128)(2,1)}), bf16[32,4,56,128]{3,2,1,0:T(8,128)(2,1)S(1)}, u32[]{:S(2)}, u32[]{:S(2)}) %all-to-all-start) | async-done | bytes 1835040 | tf_op jit(solution)/shard_map/all_to_all | solution.py:249
  60.2 1.0 copy.94
  61.2 1.0 copy.95
  62.2 1.0 collective-permute-start.9
  63.2 1.0 collective-permute-start.10
  64.4 1.0 copy.96
  65.4 1.0 copy.97
  66.9 1.6 collective-permute-start.8
  68.5 0.9 copy-done.4
  69.4 1.5 copy.60.refs_0_
  71.0 0.6 scatter_custom_fusion
  71.9 0.8 maximum_select_fusion
  72.7 0.6 broadcast_in_dim.27.refs_12_
  73.3 4.0 %pieces_here.1 = bf16[2,4,768,256]{3,2,1,0:T(8,128)(2,1)S(1)} custom-call(s32[3]{0:T(128)S(1)} %pad_add_fusion.1.place, bf16[32,4,56,128]{3,2,1,0:T(8,128)(2,1)S(1)} %all-to-all-done.refs_0_), custom_call_target="tpu_custom_call" | custom-call | bytes 16777216 | tf_op jit(solution)/shard_map/pieces_here/pallas_call | solution.py:268
  77.4 12.4 %collective-permute-done.6.refs_1_ = bf16[1024,384]{1,0:T(8,128)(2,1)} collective-permute-done((bf16[1024,384]{1,0:T(8,128)(2,1)S(1)}, bf16[1024,384]{1,0:T(8,128)(2,1)}, u32[]{:S(2)}, u32[]{:S(2)}) %collective-permute-start.6) | collective-permute-done | bytes 786464 | tf_op jit(solution)/shard_map/ppermute | solution.py:280
  89.7 0.7 collective-permute-done.8.refs_1_
  90.5 1.2 fusion.15
  91.9 1.3 collective-permute-start.11
  93.2 0.9 collective-permute-start.12
  94.1 1.2 collective-permute-start.5
  95.3 2.0 %collective-permute-start.13 = (bf16[1024,384]{1,0:T(8,128)(2,1)}, bf16[1024,384]{1,0:T(8,128)(2,1)S(1)}, u32[]{:S(2)}, u32[]{:S(2)}) collective-permute-start(bf16[1024,384]{1,0:T(8,128)(2,1)} %collective-permute-done.6.refs_1_), channel_id=1, source_target_pairs={{0,6},{2,0},{4,2},{6,4},{1,7},{3,1},{5,3},{7,5},{8,14},{10,8},{12,... | collective-permute-start | bytes 2359304 | tf_op jit(solution)/shard_map/ppermute | solution.py:290
  97.3 4.7 %pieces_z.1 = bf16[2,4,768,256]{3,2,1,0:T(8,128)(2,1)S(1)} custom-call(s32[3]{0:T(128)S(1)} %pad_add_fusion.1.place, bf16[2,32,56,128]{3,2,1,0:T(8,128)(2,1)S(1)} %collective-permute-done.9.refs_0_, bf16[2,32,56,128]{3,2,1,0:T(8,128)(2,1)} %collective-permute-done.10.refs_1_), custom_call_target="tpu_custom_call" | custom-call | bytes 16777216 | tf_op jit(solution)/shard_map/pieces_z/pallas_call | solution.py:268
  102.0 1.6 copy-done
  103.7 4.9 %pieces_x.1 = bf16[2,4,768,256]{3,2,1,0:T(8,128)(2,1)S(1)} custom-call(s32[3]{0:T(128)S(1)} %pad_add_fusion.1.place, bf16[2,32,56,128]{3,2,1,0:T(8,128)(2,1)} %collective-permute-done.7.refs_0_, bf16[2,32,56,128]{3,2,1,0:T(8,128)(2,1)} %collective-permute-done.8.refs_1_), custom_call_target="tpu_custom_call" | custom-call | bytes 16777216 | tf_op jit(solution)/shard_map/pieces_x/pallas_call | solution.py:268
  108.6 1.7 copy-done.1
  110.3 2.8 %collective-permute-done.5.refs_3_ = bf16[1024,384]{1,0:T(8,128)(2,1)S(1)} collective-permute-done((bf16[1024,384]{1,0:T(8,128)(2,1)S(1)}, bf16[1024,384]{1,0:T(8,128)(2,1)S(1)}, u32[]{:S(2)}, u32[]{:S(2)}) %collective-permute-start.5) | collective-permute-done | bytes 786464 | tf_op jit(solution)/shard_map/ppermute | solution.py:290
  113.6 1.4 collective-permute-done.12.refs_1_
  115.1 4.0 %pieces_diagonal.1 = bf16[2,4,768,256]{3,2,1,0:T(8,128)(2,1)S(1)} custom-call(s32[3]{0:T(128)S(1)} %pad_add_fusion.1.place, bf16[2,32,56,128]{3,2,1,0:T(8,128)(2,1)S(1)} %collective-permute-done.11.refs_0_, bf16[2,32,56,128]{3,2,1,0:T(8,128)(2,1)S(1)} %collective-permute-done.12.refs_1_), custom_call_target="tpu_custom_call" | custom-call | bytes 16777216 | tf_op jit(solution)/shard_map/pieces_diagonal/pallas_call | solution.py:268
  119.1 1.7 copy-done.2
  120.8 17.7 %hidden.1 = (bf16[16,192,512]{2,1,0:T(8,128)(2,1)S(1)}, bf16[1024,1024]{1,0:T(8,128)(2,1)S(1)}, bf16[4,2,192,1024]{3,2,1,0:T(8,128)(2,1)S(1)}) custom-call(s32[33]{0:T(128)S(1)} %pad_add_fusion.2.tab, bf16[1024,384]{1,0:T(8,128)(2,1)S(1)} %copy.60.refs_0_, bf16[1024,384]{1,0:T(8,128)(2,1)} %collective-permute-done.6.refs_1_, ...), custom_call_target="tpu_custom_call" | custom-call | tf_op jit(solution)/shard_map/hidden/pallas_call | solution.py:305
  138.6 0.6 collective-permute-start.17
  139.1 4.1 %own_side.1 = bf16[16,192,512]{2,1,0:T(8,128)(2,1)S(1)} custom-call(bf16[4,2,192,1024]{3,2,1,0:T(8,128)(2,1)S(1)} %get-tuple-element.64.wd, bf16[1024,1024]{1,0:T(8,128)(2,1)S(1)} %get-tuple-element.65.hid), custom_call_target="tpu_custom_call" | custom-call | flops 3221225472 | bytes 8388608 | tf_op jit(solution)/shard_map/own_side/pallas_call | solution.py:326
  143.3 1.2 collective-permute-done.17
  144.4 1.1 add_convert_fusion
  145.6 47.4 %all_to_all.10 = bf16[16,192,512]{2,1,0:T(8,128)(2,1)S(1)} all-to-all(bf16[16,192,512]{2,1,0:T(8,128)(2,1)S(1)} %add_convert_fusion), channel_id=1, replica_groups=mesh['zl'=2,'xh'=2,'xl'=2,'zh'=2,'y'=4,'core'=2] {'xh','zh','y'}, dimensions={0} | all-to-all | bytes 6291456 | tf_op jit(solution)/shard_map/all_to_all | solution.py:337
  193.4 0.7 reshape.196
  (58 shorter events, 4.3 us)
Async XLA Ops:
  1.0 21.3 %collective-permute-start.1 = (bf16[192,512]{1,0:T(8,128)(2,1)S(1)}, bf16[192,512]{1,0:T(8,128)(2,1)S(1)}, u32[]{:S(2)}, u32[]{:S(2)}) collective-permute-start(bf16[192,512]{1,0:T(8,128)(2,1)S(1)} %bitcast.68), channel_id=1, source_target_pairs={{0,8},{8,0},{1,9},{9,1},{2,10},{10,2},{3,11},{11,3},{4,12},{12,4},... | collective-permute-start | bytes 589832 | tf_op jit(solution)/shard_map/ppermute | solution.py:217
  4.1 11.4 %collective-permute-start = (bf16[192,512]{1,0:T(8,128)(2,1)S(1)}, bf16[192,512]{1,0:T(8,128)(2,1)S(1)}, u32[]{:S(2)}, u32[]{:S(2)}) collective-permute-start(bf16[192,512]{1,0:T(8,128)(2,1)S(1)} %bitcast.69), channel_id=1, source_target_pairs={{0,32},{32,0},{1,33},{33,1},{2,34},{34,2},{3,35},{35,3},{4,36},{36... | collective-permute-start | bytes 589832 | tf_op jit(solution)/shard_map/ppermute | solution.py:217
  14.8 0.7 copy-start.9
  14.8 0.7 copy-start.10
  15.5 7.7 %copy-start.7 = (f32[4,512]{1,0:T(4,128)}, f32[4,512]{1,0:T(4,128)S(1)}, u32[]{:S(2)}) copy-start(f32[4,512]{1,0:T(4,128)S(1)} %select_reduce_fusion) | copy-start | bytes 24580
  15.5 7.7 %collective-permute-start.2 = (bf16[192,512]{1,0:T(8,128)(2,1)S(1)}, bf16[192,512]{1,0:T(8,128)(2,1)S(1)}, u32[]{:S(2)}, u32[]{:S(2)}) collective-permute-start(bf16[192,512]{1,0:T(8,128)(2,1)S(1)} %collective-permute-done), channel_id=1, source_target_pairs={{0,8},{8,0},{1,9},{9,1},{2,10},{10,2},{3,11},{11,3},{4,12},{12,4},... | collective-permute-start | bytes 589832 | tf_op jit(solution)/shard_map/ppermute | solution.py:229
  16.2 6.2 %collective-permute-start.3 = (f32[4,512]{1,0:T(4,128)S(1)}, f32[4,512]{1,0:T(4,128)S(1)}, u32[]{:S(2)}, u32[]{:S(2)}) collective-permute-start(f32[4,512]{1,0:T(4,128)S(1)} %select_reduce_fusion), channel_id=1, source_target_pairs={{0,32},{32,0},{1,33},{33,1},{2,34},{34,2},{3,35},{35,3},{4,36},{36... | collective-permute-start | bytes 24584 | tf_op jit(solution)/shard_map/ppermute | solution.py:230
  21.1 1.3 copy-start.3
  22.3 0.9 copy-start.8
  23.2 36.8 %all-to-all-start = ((bf16[32,4,56,128]{3,2,1,0:T(8,128)(2,1)}), bf16[32,4,56,128]{3,2,1,0:T(8,128)(2,1)S(1)}, u32[]{:S(2)}, u32[]{:S(2)}) async-start(bf16[32,4,56,128]{3,2,1,0:T(8,128)(2,1)} %copy-done.3), calls=%async_computation | async-start | bytes 3670016 | tf_op jit(solution)/shard_map/all_to_all | solution.py:249
  33.9 0.9 copy-start.6
  36.0 32.5 %collective-permute-start.4 = (bf16[1024,384]{1,0:T(8,128)(2,1)}, bf16[1024,384]{1,0:T(8,128)(2,1)S(1)}, u32[]{:S(2)}, u32[]{:S(2)}) collective-permute-start(bf16[1024,384]{1,0:T(8,128)(2,1)} %copy.53), channel_id=1, source_target_pairs={{0,1},{1,0},{2,3},{3,2},{4,5},{5,4},{6,7},{7,6},{8,9},{9,8},{10,11... | collective-permute-start | bytes 2359304 | tf_op jit(solution)/shard_map/ppermute | solution.py:278
  62.2 27.5 %collective-permute-start.9 = (bf16[2,32,56,128]{3,2,1,0:T(8,128)(2,1)}, bf16[2,32,56,128]{3,2,1,0:T(8,128)(2,1)S(1)}, u32[]{:S(2)}, u32[]{:S(2)}) collective-permute-start(bf16[2,32,56,128]{3,2,1,0:T(8,128)(2,1)} %bitcast.53), channel_id=1, source_target_pairs={{64,0},{8,64},{72,8},{0,72},{65,1},{9,65},{73,9},{1,73},{66,2},{10... | collective-permute-start | bytes 2752520 | tf_op jit(solution)/shard_map/ppermute | solution.py:261
  63.2 26.5 %collective-permute-start.10 = (bf16[2,32,56,128]{3,2,1,0:T(8,128)(2,1)}, bf16[2,32,56,128]{3,2,1,0:T(8,128)(2,1)}, u32[]{:S(2)}, u32[]{:S(2)}) collective-permute-start(bf16[2,32,56,128]{3,2,1,0:T(8,128)(2,1)} %bitcast.52), channel_id=1, source_target_pairs={{0,64},{64,8},{8,72},{72,0},{1,65},{65,9},{9,73},{73,1},{2,66},{66... | collective-permute-start | bytes 2752520 | tf_op jit(solution)/shard_map/ppermute | solution.py:261
  64.4 6.6 %copy-start.11 = (s32[16]{0:T(128)S(1)}, s32[16]{0:T(128)}, u32[]{:S(2)}) copy-start(s32[16]{0:T(128)} %param.12) | copy-start | bytes 196
  66.4 23.3 %collective-permute-start.7 = (bf16[2,32,56,128]{3,2,1,0:T(8,128)(2,1)}, bf16[2,32,56,128]{3,2,1,0:T(8,128)(2,1)}, u32[]{:S(2)}, u32[]{:S(2)}) collective-permute-start(bf16[2,32,56,128]{3,2,1,0:T(8,128)(2,1)} %bitcast.55), channel_id=1, source_target_pairs={{0,48},{16,0},{32,16},{48,32},{1,49},{17,1},{33,17},{49,33},{2,50}... | collective-permute-start | bytes 2752520 | tf_op jit(solution)/shard_map/ppermute | solution.py:258
  66.9 23.6 %collective-permute-start.8 = (bf16[2,32,56,128]{3,2,1,0:T(8,128)(2,1)}, bf16[2,32,56,128]{3,2,1,0:T(8,128)(2,1)}, u32[]{:S(2)}, u32[]{:S(2)}) collective-permute-start(bf16[2,32,56,128]{3,2,1,0:T(8,128)(2,1)} %bitcast.54), channel_id=1, source_target_pairs={{0,16},{16,32},{32,48},{48,0},{1,17},{17,33},{33,49},{49,1},{2,18}... | collective-permute-start | bytes 2752520 | tf_op jit(solution)/shard_map/ppermute | solution.py:258
  68.5 0.9 copy-start.4
  70.9 18.8 %collective-permute-start.6 = (bf16[1024,384]{1,0:T(8,128)(2,1)S(1)}, bf16[1024,384]{1,0:T(8,128)(2,1)}, u32[]{:S(2)}, u32[]{:S(2)}) collective-permute-start(bf16[1024,384]{1,0:T(8,128)(2,1)S(1)} %copy.60.refs_0_), channel_id=1, source_target_pairs={{0,6},{2,0},{4,2},{6,4},{1,7},{3,1},{5,3},{7,5},{8,14},{10,8},{12,... | collective-permute-start | bytes 2359304 | tf_op jit(solution)/shard_map/ppermute | solution.py:280
  91.9 21.8 %collective-permute-start.11 = (bf16[2,32,56,128]{3,2,1,0:T(8,128)(2,1)S(1)}, bf16[2,32,56,128]{3,2,1,0:T(8,128)(2,1)S(1)}, u32[]{:S(2)}, u32[]{:S(2)}) collective-permute-start(bf16[2,32,56,128]{3,2,1,0:T(8,128)(2,1)S(1)} %pad_maximum_fusion), channel_id=1, source_target_pairs={{0,48},{16,0},{32,16},{48,32},{1,49},{17,1},{33,17},{49,33},{2,50}... | collective-permute-start | bytes 2752520 | tf_op jit(solution)/shard_map/ppermute | solution.py:258
  93.2 21.9 %collective-permute-start.12 = (bf16[2,32,56,128]{3,2,1,0:T(8,128)(2,1)S(1)}, bf16[2,32,56,128]{3,2,1,0:T(8,128)(2,1)S(1)}, u32[]{:S(2)}, u32[]{:S(2)}) collective-permute-start(bf16[2,32,56,128]{3,2,1,0:T(8,128)(2,1)S(1)} %pad_maximum_fusion.1), channel_id=1, source_target_pairs={{0,16},{16,32},{32,48},{48,0},{1,17},{17,33},{33,49},{49,1},{2,18}... | collective-permute-start | bytes 2752520 | tf_op jit(solution)/shard_map/ppermute | solution.py:258
  94.1 19.0 %collective-permute-start.5 = (bf16[1024,384]{1,0:T(8,128)(2,1)S(1)}, bf16[1024,384]{1,0:T(8,128)(2,1)S(1)}, u32[]{:S(2)}, u32[]{:S(2)}) collective-permute-start(bf16[1024,384]{1,0:T(8,128)(2,1)S(1)} %copy.60.refs_0_), channel_id=1, source_target_pairs={{0,2},{2,4},{4,6},{6,0},{1,3},{3,5},{5,7},{7,1},{8,10},{10,12},{12... | collective-permute-start | bytes 2359304 | tf_op jit(solution)/shard_map/ppermute | solution.py:290
  95.3 18.3 %collective-permute-start.13 = (bf16[1024,384]{1,0:T(8,128)(2,1)}, bf16[1024,384]{1,0:T(8,128)(2,1)S(1)}, u32[]{:S(2)}, u32[]{:S(2)}) collective-permute-start(bf16[1024,384]{1,0:T(8,128)(2,1)} %collective-permute-done.6.refs_1_), channel_id=1, source_target_pairs={{0,6},{2,0},{4,2},{6,4},{1,7},{3,1},{5,3},{7,5},{8,14},{10,8},{12,... | collective-permute-start | bytes 2359304 | tf_op jit(solution)/shard_map/ppermute | solution.py:290
  102.0 1.6 copy-start
  108.6 1.7 copy-start.1
  110.3 10.5 %copy-start.5 = (bf16[1024,384]{1,0:T(8,128)(2,1)S(1)}, bf16[1024,384]{1,0:T(8,128)(2,1)}, u32[]{:S(2)}) copy-start(bf16[1024,384]{1,0:T(8,128)(2,1)} %copy-done.4) | copy-start | bytes 2359300
  113.1 7.7 %collective-permute-start.14 = (bf16[1024,384]{1,0:T(8,128)(2,1)}, bf16[1024,384]{1,0:T(8,128)(2,1)S(1)}, u32[]{:S(2)}, u32[]{:S(2)}) collective-permute-start(bf16[1024,384]{1,0:T(8,128)(2,1)} %collective-permute-done.6.refs_1_), channel_id=1, source_target_pairs={{0,1},{1,0},{2,3},{3,2},{4,5},{5,4},{6,7},{7,6},{8,9},{9,8},{10,11... | collective-permute-start | bytes 2359304 | tf_op jit(solution)/shard_map/ppermute | solution.py:293
  113.1 7.7 %collective-permute-start.16 = (bf16[1024,384]{1,0:T(8,128)(2,1)S(1)}, bf16[1024,384]{1,0:T(8,128)(2,1)S(1)}, u32[]{:S(2)}, u32[]{:S(2)}) collective-permute-start(bf16[1024,384]{1,0:T(8,128)(2,1)S(1)} %collective-permute-done.5.refs_3_), channel_id=1, source_target_pairs={{0,1},{1,0},{2,3},{3,2},{4,5},{5,4},{6,7},{7,6},{8,9},{9,8},{10,11... | collective-permute-start | bytes 2359304 | tf_op jit(solution)/shard_map/ppermute | solution.py:293
  115.1 5.7 %collective-permute-start.15 = (bf16[1024,384]{1,0:T(8,128)(2,1)S(1)}, bf16[1024,384]{1,0:T(8,128)(2,1)S(1)}, u32[]{:S(2)}, u32[]{:S(2)}) collective-permute-start(bf16[1024,384]{1,0:T(8,128)(2,1)S(1)} %collective-permute-done.13.refs_2_), channel_id=1, source_target_pairs={{0,1},{1,0},{2,3},{3,2},{4,5},{5,4},{6,7},{7,6},{8,9},{9,8},{10,11... | collective-permute-start | bytes 2359304 | tf_op jit(solution)/shard_map/ppermute | solution.py:295
  119.1 1.7 copy-start.2
  138.6 5.9 %collective-permute-start.17 = (bf16[16,192,512]{2,1,0:T(8,128)(2,1)S(1)}, bf16[16,192,512]{2,1,0:T(8,128)(2,1)S(1)}, u32[]{:S(2)}, u32[]{:S(2)}) collective-permute-start(bf16[16,192,512]{2,1,0:T(8,128)(2,1)S(1)} %get-tuple-element.66), channel_id=1, source_target_pairs={{0,1},{1,0},{2,3},{3,2},{4,5},{5,4},{6,7},{7,6},{8,9},{9,8},{10,11... | collective-permute-start | bytes 9437192 | tf_op jit(solution)/shard_map/ppermute | solution.py:325

commit v5 on v4

--- a/solution.py
+++ b/solution.py
@@ -164,13 +164,15 @@
             lanes = pl.ds(pl.multiple_of(side * HALF + ((y + n) % 4) * 384, 128), 384)
             gets.append(pltpu.make_async_copy(ref, x.at[:, lanes], xsem.at[len(gets)]))
             gets[-1].start()
-    fetch_pieces(tab, ws, 0, (0, EXPERTS), start)
-    gets.append(pltpu.make_async_copy(mix_ref, mix, msem))
-    gets[-1].start()
+    fetch_pieces(tab, ws, 0, (0, 1), start)
+    get_mix = pltpu.make_async_copy(mix_ref, mix, msem)
+    for get in gets:
+        get.wait()
+    get_mix.start()
+    fetch_pieces(tab, ws, 0, (1, EXPERTS), start)
     fetch_down(tab, ws, wd, dsem.at[1], 1)
     fetch_down(tab, ws, wd_own, dsem.at[0], 0)
-    for get in gets:
-        get.wait()
+    get_mix.wait()
 
     lanes = lax.broadcasted_iota(jnp.int32, (2 * TOK, 128), 1) % 64
 

time: 195 us -> 195 us (level)
  no operation moved by 1% of the time
where the time goes in v5:
time: 195 us; the launch traced here: 194 us
  blocking collectives  47.4 us (24%)
  Pallas kernels  43.8 us (22%)
  waiting for transfers between devices  43.2 us (22%)
  starting transfers between devices  27.6 us (14%)
  local copies, waits for them, and re-layouts  21.2 us (11%)
  other arithmetic  10.6 us (5%)
    all_to_all x1, blocking collectives, shards(): parts = lax.all_to_all(both, chips, 0, 0)  47.4 us
    all_to_all x1, waiting for transfers between devices, shards(): w0 = lax.all_to_all(packed, ('xh', 'zh', 'y', 'core'), 0, 0)  23.8 us
    pallas_call x1, Pallas kernels, shards(): pl.pallas_call(hidden_kernel, out_shape=[sums, hidden, down_half], in_spe...  17.8 us
    pallas_call x4, Pallas kernels, assemble(): pl.pallas_call(functools.partial(assemble_kernel, name != 'pieces_z'), ou...  17.6 us
    unnamed x29, local copies, waits for them, and re-layouts  12.7 us
    ppermute x1, waiting for transfers between devices, shards(): above = lax.ppermute(held, 'y', minus)  12.4 us
    all_to_all x1, starting transfers between devices, shards(): w0 = lax.all_to_all(packed, ('xh', 'zh', 'y', 'core'), 0, 0)  9.46 us
    transpose x1, other arithmetic, update(): updated.transpose(0, 2, 1, 3)  7.67 us
  transfers between devices with their start and end apart: 19, of which 7 were waited for; matrix products, arithmetic and copies ran while one was open for 10% of the time, Pallas kernels for 13%

profile of v5, /device:TPU:32, one launch (start us, length us, event | category | flops | bytes accessed | tf_op | source)
XLA Modules:
  0.0 194.2 jit_solution(429224584829563770)
XLA Ops:
  0.0 1.0 reshape.185
  1.0 3.1 %collective-permute-start.1 = (bf16[192,512]{1,0:T(8,128)(2,1)S(1)}, bf16[192,512]{1,0:T(8,128)(2,1)S(1)}, u32[]{:S(2)}, u32[]{:S(2)}) collective-permute-start(bf16[192,512]{1,0:T(8,128)(2,1)S(1)} %bitcast.68), channel_id=1, source_target_pairs={{0,8},{8,0},{1,9},{9,1},{2,10},{10,2},{3,11},{11,3},{4,12},{12,4},... | collective-permute-start | bytes 589832 | tf_op jit(solution)/shard_map/ppermute | solution.py:219
  4.1 3.0 %collective-permute-start = (bf16[192,512]{1,0:T(8,128)(2,1)S(1)}, bf16[192,512]{1,0:T(8,128)(2,1)S(1)}, u32[]{:S(2)}, u32[]{:S(2)}) collective-permute-start(bf16[192,512]{1,0:T(8,128)(2,1)S(1)} %bitcast.69), channel_id=1, source_target_pairs={{0,32},{32,0},{1,33},{33,1},{2,34},{34,2},{3,35},{35,3},{4,36},{36... | collective-permute-start | bytes 589832 | tf_op jit(solution)/shard_map/ppermute | solution.py:219
  7.1 7.7 %fusion.8 = bf16[2,3,45,2880]{3,2,1,0:T(8,128)(2,1)S(1)} fusion(f32[2,45,3,2880]{3,0,2,1:T(2,128)} %param.10, f32[2,45,3,2880]{3,0,2,1:T(2,128)} %param.11, f32[2,45,3,2880]{3,0,2,1:T(2,128)} %param.9, f32[2,45,3,2880]{3,0,2,1:T(2,128)} %param.8), kind=kLoop, calls=%fused_computation.14 | loop fusion | flops 12441600 | bytes 13996800 | tf_op jit(solution)/shard_map/transpose | solution.py:206
  15.5 0.6 collective-permute-start.2
  16.7 4.3 %pack.1 = bf16[32,4,56,128]{3,2,1,0:T(8,128)(2,1)S(1)} custom-call(s32[3]{0:T(128)S(1)} %pad_add_fusion.1.place, bf16[2,3,48,3072]{3,2,1,0:T(8,128)(2,1)S(1)} %pad.8.w_ref), custom_call_target="tpu_custom_call" | custom-call | tf_op jit(solution)/shard_map/pack/pallas_call | solution.py:242
  21.1 1.2 copy-done.3
  22.3 0.9 collective-permute-done.2
  23.2 9.5 %all-to-all-start = ((bf16[32,4,56,128]{3,2,1,0:T(8,128)(2,1)}), bf16[32,4,56,128]{3,2,1,0:T(8,128)(2,1)S(1)}, u32[]{:S(2)}, u32[]{:S(2)}) async-start(bf16[32,4,56,128]{3,2,1,0:T(8,128)(2,1)} %copy-done.3), calls=%async_computation | async-start | bytes 3670016 | tf_op jit(solution)/shard_map/all_to_all | solution.py:251
  32.9 0.8 copy.52
  33.9 0.9 copy-done.6
  34.7 1.2 copy.53
  36.2 23.8 %all-to-all-done.refs_0_ = bf16[32,4,56,128]{3,2,1,0:T(8,128)(2,1)S(1)} async-done(((bf16[32,4,56,128]{3,2,1,0:T(8,128)(2,1)}), bf16[32,4,56,128]{3,2,1,0:T(8,128)(2,1)S(1)}, u32[]{:S(2)}, u32[]{:S(2)}) %all-to-all-start) | async-done | bytes 1835040 | tf_op jit(solution)/shard_map/all_to_all | solution.py:251
  60.2 1.0 copy.94
  61.2 1.0 copy.95
  62.2 1.0 collective-permute-start.9
  63.2 1.0 collective-permute-start.10
  64.4 1.0 copy.96
  65.4 1.0 copy.97
  66.9 1.6 collective-permute-start.8
  68.5 0.9 copy-done.4
  69.4 1.5 copy.60.refs_0_
  71.0 0.6 scatter_custom_fusion
  71.9 0.8 maximum_select_fusion
  72.7 0.6 broadcast_in_dim.27.refs_12_
  73.3 4.0 %pieces_here.1 = bf16[2,4,768,256]{3,2,1,0:T(8,128)(2,1)S(1)} custom-call(s32[3]{0:T(128)S(1)} %pad_add_fusion.1.place, bf16[32,4,56,128]{3,2,1,0:T(8,128)(2,1)S(1)} %all-to-all-done.refs_0_), custom_call_target="tpu_custom_call" | custom-call | bytes 16777216 | tf_op jit(solution)/shard_map/pieces_here/pallas_call | solution.py:270
  77.4 12.4 %collective-permute-done.6.refs_1_ = bf16[1024,384]{1,0:T(8,128)(2,1)} collective-permute-done((bf16[1024,384]{1,0:T(8,128)(2,1)S(1)}, bf16[1024,384]{1,0:T(8,128)(2,1)}, u32[]{:S(2)}, u32[]{:S(2)}) %collective-permute-start.6) | collective-permute-done | bytes 786464 | tf_op jit(solution)/shard_map/ppermute | solution.py:282
  89.7 0.7 collective-permute-done.8.refs_1_
  90.5 1.2 fusion.15
  91.9 1.3 collective-permute-start.11
  93.2 0.9 collective-permute-start.12
  94.1 1.2 collective-permute-start.5
  95.3 2.0 %collective-permute-start.13 = (bf16[1024,384]{1,0:T(8,128)(2,1)}, bf16[1024,384]{1,0:T(8,128)(2,1)S(1)}, u32[]{:S(2)}, u32[]{:S(2)}) collective-permute-start(bf16[1024,384]{1,0:T(8,128)(2,1)} %collective-permute-done.6.refs_1_), channel_id=1, source_target_pairs={{0,6},{2,0},{4,2},{6,4},{1,7},{3,1},{5,3},{7,5},{8,14},{10,8},{12,... | collective-permute-start | bytes 2359304 | tf_op jit(solution)/shard_map/ppermute | solution.py:292
  97.3 4.7 %pieces_z.1 = bf16[2,4,768,256]{3,2,1,0:T(8,128)(2,1)S(1)} custom-call(s32[3]{0:T(128)S(1)} %pad_add_fusion.1.place, bf16[2,32,56,128]{3,2,1,0:T(8,128)(2,1)S(1)} %collective-permute-done.9.refs_0_, bf16[2,32,56,128]{3,2,1,0:T(8,128)(2,1)} %collective-permute-done.10.refs_1_), custom_call_target="tpu_custom_call" | custom-call | bytes 16777216 | tf_op jit(solution)/shard_map/pieces_z/pallas_call | solution.py:270
  102.0 1.6 copy-done
  103.7 4.9 %pieces_x.1 = bf16[2,4,768,256]{3,2,1,0:T(8,128)(2,1)S(1)} custom-call(s32[3]{0:T(128)S(1)} %pad_add_fusion.1.place, bf16[2,32,56,128]{3,2,1,0:T(8,128)(2,1)} %collective-permute-done.7.refs_0_, bf16[2,32,56,128]{3,2,1,0:T(8,128)(2,1)} %collective-permute-done.8.refs_1_), custom_call_target="tpu_custom_call" | custom-call | bytes 16777216 | tf_op jit(solution)/shard_map/pieces_x/pallas_call | solution.py:270
  108.6 1.7 copy-done.1
  110.3 2.8 %collective-permute-done.5.refs_3_ = bf16[1024,384]{1,0:T(8,128)(2,1)S(1)} collective-permute-done((bf16[1024,384]{1,0:T(8,128)(2,1)S(1)}, bf16[1024,384]{1,0:T(8,128)(2,1)S(1)}, u32[]{:S(2)}, u32[]{:S(2)}) %collective-permute-start.5) | collective-permute-done | bytes 786464 | tf_op jit(solution)/shard_map/ppermute | solution.py:292
  113.6 1.4 collective-permute-done.12.refs_1_
  115.1 4.0 %pieces_diagonal.1 = bf16[2,4,768,256]{3,2,1,0:T(8,128)(2,1)S(1)} custom-call(s32[3]{0:T(128)S(1)} %pad_add_fusion.1.place, bf16[2,32,56,128]{3,2,1,0:T(8,128)(2,1)S(1)} %collective-permute-done.11.refs_0_, bf16[2,32,56,128]{3,2,1,0:T(8,128)(2,1)S(1)} %collective-permute-done.12.refs_1_), custom_call_target="tpu_custom_call" | custom-call | bytes 16777216 | tf_op jit(solution)/shard_map/pieces_diagonal/pallas_call | solution.py:270
  119.1 1.7 copy-done.2
  120.8 17.8 %hidden.1 = (bf16[16,192,512]{2,1,0:T(8,128)(2,1)S(1)}, bf16[1024,1024]{1,0:T(8,128)(2,1)S(1)}, bf16[4,2,192,1024]{3,2,1,0:T(8,128)(2,1)S(1)}) custom-call(s32[33]{0:T(128)S(1)} %pad_add_fusion.2.tab, bf16[1024,384]{1,0:T(8,128)(2,1)S(1)} %copy.60.refs_0_, bf16[1024,384]{1,0:T(8,128)(2,1)} %collective-permute-done.6.refs_1_, ...), custom_call_target="tpu_custom_call" | custom-call | tf_op jit(solution)/shard_map/hidden/pallas_call | solution.py:307
  138.6 0.6 collective-permute-start.17
  139.2 4.1 %own_side.1 = bf16[16,192,512]{2,1,0:T(8,128)(2,1)S(1)} custom-call(bf16[4,2,192,1024]{3,2,1,0:T(8,128)(2,1)S(1)} %get-tuple-element.64.wd, bf16[1024,1024]{1,0:T(8,128)(2,1)S(1)} %get-tuple-element.65.hid), custom_call_target="tpu_custom_call" | custom-call | flops 3221225472 | bytes 8388608 | tf_op jit(solution)/shard_map/own_side/pallas_call | solution.py:328
  143.3 1.2 collective-permute-done.17
  144.4 1.1 add_convert_fusion
  145.6 47.4 %all_to_all.10 = bf16[16,192,512]{2,1,0:T(8,128)(2,1)S(1)} all-to-all(bf16[16,192,512]{2,1,0:T(8,128)(2,1)S(1)} %add_convert_fusion), channel_id=1, replica_groups=mesh['zl'=2,'xh'=2,'xl'=2,'zh'=2,'y'=4,'core'=2] {'xh','zh','y'}, dimensions={0} | all-to-all | bytes 6291456 | tf_op jit(solution)/shard_map/all_to_all | solution.py:339
  193.4 0.7 reshape.196
  (58 shorter events, 4.3 us)
Async XLA Ops:
  1.0 21.3 %collective-permute-start.1 = (bf16[192,512]{1,0:T(8,128)(2,1)S(1)}, bf16[192,512]{1,0:T(8,128)(2,1)S(1)}, u32[]{:S(2)}, u32[]{:S(2)}) collective-permute-start(bf16[192,512]{1,0:T(8,128)(2,1)S(1)} %bitcast.68), channel_id=1, source_target_pairs={{0,8},{8,0},{1,9},{9,1},{2,10},{10,2},{3,11},{11,3},{4,12},{12,4},... | collective-permute-start | bytes 589832 | tf_op jit(solution)/shard_map/ppermute | solution.py:219
  4.1 11.4 %collective-permute-start = (bf16[192,512]{1,0:T(8,128)(2,1)S(1)}, bf16[192,512]{1,0:T(8,128)(2,1)S(1)}, u32[]{:S(2)}, u32[]{:S(2)}) collective-permute-start(bf16[192,512]{1,0:T(8,128)(2,1)S(1)} %bitcast.69), channel_id=1, source_target_pairs={{0,32},{32,0},{1,33},{33,1},{2,34},{34,2},{3,35},{35,3},{4,36},{36... | collective-permute-start | bytes 589832 | tf_op jit(solution)/shard_map/ppermute | solution.py:219
  14.8 0.7 copy-start.9
  14.8 0.7 copy-start.10
  15.5 7.7 %copy-start.7 = (f32[4,512]{1,0:T(4,128)}, f32[4,512]{1,0:T(4,128)S(1)}, u32[]{:S(2)}) copy-start(f32[4,512]{1,0:T(4,128)S(1)} %select_reduce_fusion) | copy-start | bytes 24580
  15.5 7.7 %collective-permute-start.2 = (bf16[192,512]{1,0:T(8,128)(2,1)S(1)}, bf16[192,512]{1,0:T(8,128)(2,1)S(1)}, u32[]{:S(2)}, u32[]{:S(2)}) collective-permute-start(bf16[192,512]{1,0:T(8,128)(2,1)S(1)} %collective-permute-done), channel_id=1, source_target_pairs={{0,8},{8,0},{1,9},{9,1},{2,10},{10,2},{3,11},{11,3},{4,12},{12,4},... | collective-permute-start | bytes 589832 | tf_op jit(solution)/shard_map/ppermute | solution.py:231
  16.2 6.2 %collective-permute-start.3 = (f32[4,512]{1,0:T(4,128)S(1)}, f32[4,512]{1,0:T(4,128)S(1)}, u32[]{:S(2)}, u32[]{:S(2)}) collective-permute-start(f32[4,512]{1,0:T(4,128)S(1)} %select_reduce_fusion), channel_id=1, source_target_pairs={{0,32},{32,0},{1,33},{33,1},{2,34},{34,2},{3,35},{35,3},{4,36},{36... | collective-permute-start | bytes 24584 | tf_op jit(solution)/shard_map/ppermute | solution.py:232
  21.1 1.3 copy-start.3
  22.3 0.9 copy-start.8
  23.2 36.8 %all-to-all-start = ((bf16[32,4,56,128]{3,2,1,0:T(8,128)(2,1)}), bf16[32,4,56,128]{3,2,1,0:T(8,128)(2,1)S(1)}, u32[]{:S(2)}, u32[]{:S(2)}) async-start(bf16[32,4,56,128]{3,2,1,0:T(8,128)(2,1)} %copy-done.3), calls=%async_computation | async-start | bytes 3670016 | tf_op jit(solution)/shard_map/all_to_all | solution.py:251
  33.9 0.9 copy-start.6
  36.0 32.5 %collective-permute-start.4 = (bf16[1024,384]{1,0:T(8,128)(2,1)}, bf16[1024,384]{1,0:T(8,128)(2,1)S(1)}, u32[]{:S(2)}, u32[]{:S(2)}) collective-permute-start(bf16[1024,384]{1,0:T(8,128)(2,1)} %copy.53), channel_id=1, source_target_pairs={{0,1},{1,0},{2,3},{3,2},{4,5},{5,4},{6,7},{7,6},{8,9},{9,8},{10,11... | collective-permute-start | bytes 2359304 | tf_op jit(solution)/shard_map/ppermute | solution.py:280
  62.2 27.5 %collective-permute-start.9 = (bf16[2,32,56,128]{3,2,1,0:T(8,128)(2,1)}, bf16[2,32,56,128]{3,2,1,0:T(8,128)(2,1)S(1)}, u32[]{:S(2)}, u32[]{:S(2)}) collective-permute-start(bf16[2,32,56,128]{3,2,1,0:T(8,128)(2,1)} %bitcast.53), channel_id=1, source_target_pairs={{64,0},{8,64},{72,8},{0,72},{65,1},{9,65},{73,9},{1,73},{66,2},{10... | collective-permute-start | bytes 2752520 | tf_op jit(solution)/shard_map/ppermute | solution.py:263
  63.2 26.5 %collective-permute-start.10 = (bf16[2,32,56,128]{3,2,1,0:T(8,128)(2,1)}, bf16[2,32,56,128]{3,2,1,0:T(8,128)(2,1)}, u32[]{:S(2)}, u32[]{:S(2)}) collective-permute-start(bf16[2,32,56,128]{3,2,1,0:T(8,128)(2,1)} %bitcast.52), channel_id=1, source_target_pairs={{0,64},{64,8},{8,72},{72,0},{1,65},{65,9},{9,73},{73,1},{2,66},{66... | collective-permute-start | bytes 2752520 | tf_op jit(solution)/shard_map/ppermute | solution.py:263
  64.4 6.6 %copy-start.11 = (s32[16]{0:T(128)S(1)}, s32[16]{0:T(128)}, u32[]{:S(2)}) copy-start(s32[16]{0:T(128)} %param.12) | copy-start | bytes 196
  66.4 23.3 %collective-permute-start.7 = (bf16[2,32,56,128]{3,2,1,0:T(8,128)(2,1)}, bf16[2,32,56,128]{3,2,1,0:T(8,128)(2,1)}, u32[]{:S(2)}, u32[]{:S(2)}) collective-permute-start(bf16[2,32,56,128]{3,2,1,0:T(8,128)(2,1)} %bitcast.55), channel_id=1, source_target_pairs={{0,48},{16,0},{32,16},{48,32},{1,49},{17,1},{33,17},{49,33},{2,50}... | collective-permute-start | bytes 2752520 | tf_op jit(solution)/shard_map/ppermute | solution.py:260
  66.9 23.6 %collective-permute-start.8 = (bf16[2,32,56,128]{3,2,1,0:T(8,128)(2,1)}, bf16[2,32,56,128]{3,2,1,0:T(8,128)(2,1)}, u32[]{:S(2)}, u32[]{:S(2)}) collective-permute-start(bf16[2,32,56,128]{3,2,1,0:T(8,128)(2,1)} %bitcast.54), channel_id=1, source_target_pairs={{0,16},{16,32},{32,48},{48,0},{1,17},{17,33},{33,49},{49,1},{2,18}... | collective-permute-start | bytes 2752520 | tf_op jit(solution)/shard_map/ppermute | solution.py:260
  68.5 0.9 copy-start.4
  70.9 18.8 %collective-permute-start.6 = (bf16[1024,384]{1,0:T(8,128)(2,1)S(1)}, bf16[1024,384]{1,0:T(8,128)(2,1)}, u32[]{:S(2)}, u32[]{:S(2)}) collective-permute-start(bf16[1024,384]{1,0:T(8,128)(2,1)S(1)} %copy.60.refs_0_), channel_id=1, source_target_pairs={{0,6},{2,0},{4,2},{6,4},{1,7},{3,1},{5,3},{7,5},{8,14},{10,8},{12,... | collective-permute-start | bytes 2359304 | tf_op jit(solution)/shard_map/ppermute | solution.py:282
  91.9 21.8 %collective-permute-start.11 = (bf16[2,32,56,128]{3,2,1,0:T(8,128)(2,1)S(1)}, bf16[2,32,56,128]{3,2,1,0:T(8,128)(2,1)S(1)}, u32[]{:S(2)}, u32[]{:S(2)}) collective-permute-start(bf16[2,32,56,128]{3,2,1,0:T(8,128)(2,1)S(1)} %pad_maximum_fusion), channel_id=1, source_target_pairs={{0,48},{16,0},{32,16},{48,32},{1,49},{17,1},{33,17},{49,33},{2,50}... | collective-permute-start | bytes 2752520 | tf_op jit(solution)/shard_map/ppermute | solution.py:260
  93.2 21.9 %collective-permute-start.12 = (bf16[2,32,56,128]{3,2,1,0:T(8,128)(2,1)S(1)}, bf16[2,32,56,128]{3,2,1,0:T(8,128)(2,1)S(1)}, u32[]{:S(2)}, u32[]{:S(2)}) collective-permute-start(bf16[2,32,56,128]{3,2,1,0:T(8,128)(2,1)S(1)} %pad_maximum_fusion.1), channel_id=1, source_target_pairs={{0,16},{16,32},{32,48},{48,0},{1,17},{17,33},{33,49},{49,1},{2,18}... | collective-permute-start | bytes 2752520 | tf_op jit(solution)/shard_map/ppermute | solution.py:260
  94.1 19.0 %collective-permute-start.5 = (bf16[1024,384]{1,0:T(8,128)(2,1)S(1)}, bf16[1024,384]{1,0:T(8,128)(2,1)S(1)}, u32[]{:S(2)}, u32[]{:S(2)}) collective-permute-start(bf16[1024,384]{1,0:T(8,128)(2,1)S(1)} %copy.60.refs_0_), channel_id=1, source_target_pairs={{0,2},{2,4},{4,6},{6,0},{1,3},{3,5},{5,7},{7,1},{8,10},{10,12},{12... | collective-permute-start | bytes 2359304 | tf_op jit(solution)/shard_map/ppermute | solution.py:292
  95.3 18.3 %collective-permute-start.13 = (bf16[1024,384]{1,0:T(8,128)(2,1)}, bf16[1024,384]{1,0:T(8,128)(2,1)S(1)}, u32[]{:S(2)}, u32[]{:S(2)}) collective-permute-start(bf16[1024,384]{1,0:T(8,128)(2,1)} %collective-permute-done.6.refs_1_), channel_id=1, source_target_pairs={{0,6},{2,0},{4,2},{6,4},{1,7},{3,1},{5,3},{7,5},{8,14},{10,8},{12,... | collective-permute-start | bytes 2359304 | tf_op jit(solution)/shard_map/ppermute | solution.py:292
  102.0 1.6 copy-start
  108.6 1.7 copy-start.1
  110.3 10.5 %copy-start.5 = (bf16[1024,384]{1,0:T(8,128)(2,1)S(1)}, bf16[1024,384]{1,0:T(8,128)(2,1)}, u32[]{:S(2)}) copy-start(bf16[1024,384]{1,0:T(8,128)(2,1)} %copy-done.4) | copy-start | bytes 2359300
  113.1 7.7 %collective-permute-start.14 = (bf16[1024,384]{1,0:T(8,128)(2,1)}, bf16[1024,384]{1,0:T(8,128)(2,1)S(1)}, u32[]{:S(2)}, u32[]{:S(2)}) collective-permute-start(bf16[1024,384]{1,0:T(8,128)(2,1)} %collective-permute-done.6.refs_1_), channel_id=1, source_target_pairs={{0,1},{1,0},{2,3},{3,2},{4,5},{5,4},{6,7},{7,6},{8,9},{9,8},{10,11... | collective-permute-start | bytes 2359304 | tf_op jit(solution)/shard_map/ppermute | solution.py:295
  113.1 7.7 %collective-permute-start.16 = (bf16[1024,384]{1,0:T(8,128)(2,1)S(1)}, bf16[1024,384]{1,0:T(8,128)(2,1)S(1)}, u32[]{:S(2)}, u32[]{:S(2)}) collective-permute-start(bf16[1024,384]{1,0:T(8,128)(2,1)S(1)} %collective-permute-done.5.refs_3_), channel_id=1, source_target_pairs={{0,1},{1,0},{2,3},{3,2},{4,5},{5,4},{6,7},{7,6},{8,9},{9,8},{10,11... | collective-permute-start | bytes 2359304 | tf_op jit(solution)/shard_map/ppermute | solution.py:295
  115.1 5.7 %collective-permute-start.15 = (bf16[1024,384]{1,0:T(8,128)(2,1)S(1)}, bf16[1024,384]{1,0:T(8,128)(2,1)S(1)}, u32[]{:S(2)}, u32[]{:S(2)}) collective-permute-start(bf16[1024,384]{1,0:T(8,128)(2,1)S(1)} %collective-permute-done.13.refs_2_), channel_id=1, source_target_pairs={{0,1},{1,0},{2,3},{3,2},{4,5},{5,4},{6,7},{7,6},{8,9},{9,8},{10,11... | collective-permute-start | bytes 2359304 | tf_op jit(solution)/shard_map/ppermute | solution.py:297
  119.1 1.7 copy-start.2
  138.6 5.9 %collective-permute-start.17 = (bf16[16,192,512]{2,1,0:T(8,128)(2,1)S(1)}, bf16[16,192,512]{2,1,0:T(8,128)(2,1)S(1)}, u32[]{:S(2)}, u32[]{:S(2)}) collective-permute-start(bf16[16,192,512]{2,1,0:T(8,128)(2,1)S(1)} %get-tuple-element.66), channel_id=1, source_target_pairs={{0,1},{1,0},{2,3},{3,2},{4,5},{5,4},{6,7},{7,6},{8,9},{9,8},{10,11... | collective-permute-start | bytes 9437192 | tf_op jit(solution)/shard_map/ppermute | solution.py:327
